TPU v7x, 128 devices: a whole 4x4x4 slice. The times are simulated.
128 devices in a mesh: seq: 16 (over z, y), head: 8 (over x, core).
Axes of the slice: x: 4, y: 4, z: 4, core: 2. Of those that a mesh axis runs over, the one named last changes fastest.
Arguments:
- prompt_hidden: bfloat16 [16384, 7168], P('seq', 'head'), may hold values from -6 to 6
- owner: int32 [16384, 1], P('seq'), may hold values from 0 to 15; in each aligned block of 1024 rows (0 to 1023, 1024 to 2047, ...) at most 128 rows name the same one
- offsets: int32 [16384], P('seq'), may hold values from 0 to 16383, as said below
- cache: bfloat16 [256, 1024, 576], P('seq')
- lengths: int32 [256], P('seq'), may hold values from 1 to 1022, 131072 in all
- new_hidden: bfloat16 [2, 256, 7168], P(None, 'seq', 'head'), may hold values from -6 to 6
- w_down: bfloat16 [7168, 2112], P('head'), may hold values from -0.0625 to 0.0625
- gain_q: bfloat16 [1536], replicated, may hold values from 0.099609375 to 1.8984375
- gain_kv: bfloat16 [512], replicated, may hold values from 0.099609375 to 1.8984375
- w_uq: bfloat16 [1536, 24576], P(None, 'head'), may hold values from -0.15625 to 0.15625
- w_uk: bfloat16 [128, 128, 512], P('head'), may hold values from -0.5 to 0.5
- w_uv: bfloat16 [128, 512, 128], P('head'), may hold values from -0.25 to 0.25
- w_out: bfloat16 [16384, 7168], P('head', 'seq'), may hold values from -0.046875 to 0.046875
Outputs:
- attended: bfloat16 [2, 256, 7168], P(None, 'head', 'seq')
Inputs may be any that keep to these rules, and one draw needn't show every extreme that they name: offsets are distinct over all prompt tokens. Among the rows of one index of seq at most 128 name one owner.
All inputs are finite; a program needn't handle non-finite values. No bound on the sum of `lengths` on one device may be relied on, other than what follows from the above.
Results may differ from a plain program's by a relative error of at most 0.03.
Values may be sent and summed in bfloat16 or wider, within the bound.
A program may use at most 256 MiB of HBM per device.

v0:
```python
import jax
import jax.numpy as jnp
from jax import lax
from jax.sharding import PartitionSpec as P

QRANK = 1536
LATENT = 512
ROPE = 64
NOPE = 128
VDIM = 128


def rms_norm(values, gain):
    return (
        values
        * lax.rsqrt(jnp.mean(values * values, -1, keepdims=True) + 1e-06)
        * gain.astype(jnp.float32)
    )


def rotate(values, places):
    half = values.shape[-1] // 2
    inverse = 10000.0 ** (-jnp.arange(half, dtype=jnp.float32) / half)
    angles = places.astype(jnp.float32)[..., None] * inverse
    first = values[..., :half]
    second = values[..., half:]
    return jnp.concatenate(
        [
            first * jnp.cos(angles) - second * jnp.sin(angles),
            second * jnp.cos(angles) + first * jnp.sin(angles),
        ],
        -1,
    )


def latent_rows(part, gain_kv, places):
    latent = rms_norm(part[..., :LATENT], gain_kv)
    shared = rotate(part[..., LATENT:], places)
    return jnp.concatenate([latent, shared], -1).astype(jnp.bfloat16)


def local(
    prompt_hidden,
    owner,
    offsets,
    cache,
    lengths,
    new_hidden,
    w_down,
    gain_q,
    gain_kv,
    w_uq,
    w_uk,
    w_uv,
    w_out,
):
    steps, req_local, width_local = new_hidden.shape
    cache_rows = cache.shape[1]
    width = cache.shape[2]
    heads_local = w_uk.shape[0]
    prompt_part = jnp.dot(prompt_hidden, w_down[:, QRANK:], preferred_element_type=jnp.float32)
    new_part = jnp.dot(
        new_hidden.reshape(steps * req_local, width_local),
        w_down,
        preferred_element_type=jnp.float32,
    )
    prompt_part, new_part = lax.psum((prompt_part, new_part), "head")
    new_part = new_part.reshape(steps, req_local, -1)
    prompt_rows = latent_rows(prompt_part, gain_kv, offsets % cache_rows)
    limit = req_local * cache_rows
    me = lax.axis_index("seq")
    all_rows, all_owner, all_offsets = (
        lax.all_gather(prompt_rows, "seq", axis=0, tiled=True),
        lax.all_gather(owner, "seq", axis=0, tiled=True),
        lax.all_gather(offsets, "seq", axis=0, tiled=True),
    )
    got_targets = jnp.where(all_owner[:, 0] == me, all_offsets, limit).astype(jnp.int32)
    positions = lengths[None, :] + jnp.arange(steps, dtype=jnp.int32)[:, None]
    new_rows = latent_rows(new_part[..., QRANK:], gain_kv, positions)
    new_targets = jnp.arange(req_local, dtype=jnp.int32)[None, :] * cache_rows + positions
    flat = cache.reshape(limit, width)
    flat = flat.at[got_targets].set(all_rows, mode="drop")
    flat = flat.at[new_targets.reshape(-1)].set(new_rows.reshape(-1, width))
    keys = flat.reshape(req_local, cache_rows, width)
    query_latent = rms_norm(new_part[..., :QRANK], gain_q).astype(jnp.bfloat16)
    query = jnp.dot(
        query_latent.reshape(steps * req_local, QRANK), w_uq, preferred_element_type=jnp.float32
    )
    query = query.reshape(steps, req_local, heads_local, NOPE + ROPE)
    q_nope = query[..., :NOPE].astype(jnp.bfloat16)
    q_rope = rotate(query[..., NOPE:], positions[:, :, None]).astype(jnp.bfloat16)
    q_lat = jnp.einsum("srhn,hnc->srhc", q_nope, w_uk, preferred_element_type=jnp.float32).astype(
        jnp.bfloat16
    )
    joined = jnp.concatenate([q_lat, q_rope], -1)
    scores = jnp.einsum(
        "srhc,rlc->srhl", joined, keys, preferred_element_type=jnp.float32
    ) / jnp.sqrt(jnp.float32(NOPE + ROPE))
    visible = (
        jnp.arange(cache_rows, dtype=jnp.int32)[None, None, None, :] <= positions[:, :, None, None]
    )
    scores = jnp.where(visible, scores, -jnp.inf)
    top = jnp.max(scores, -1, keepdims=True)
    expo = jnp.exp(scores - top)
    weights = (expo / jnp.sum(expo, -1, keepdims=True)).astype(jnp.bfloat16)
    o_full = jnp.einsum("srhl,rlc->srhc", weights, keys, preferred_element_type=jnp.float32)
    o_lat = o_full[..., :LATENT].astype(jnp.bfloat16)
    heads_out = jnp.einsum(
        "srhc,hcv->srhv", o_lat, w_uv, preferred_element_type=jnp.float32
    ).astype(jnp.bfloat16)
    heads_out = heads_out.reshape(steps, req_local, heads_local * VDIM)
    terms = jnp.einsum(
        "srk,kd->srd",
        lax.all_gather(heads_out, "seq", axis=1, tiled=True),
        w_out,
        preferred_element_type=jnp.float32,
    )
    return lax.psum_scatter(terms.astype(jnp.bfloat16), "head", scatter_dimension=1, tiled=True)


def solution(mesh):
    in_specs = (
        P("seq", "head"),
        P("seq", None),
        P("seq"),
        P("seq", None, None),
        P("seq"),
        P(None, "seq", "head"),
        P("head", None),
        P(),
        P(),
        P(None, "head"),
        P("head", None, None),
        P("head", None, None),
        P("head", "seq"),
    )
    out_specs = P(None, "head", "seq")
    return jax.shard_map(local, mesh=mesh, in_specs=in_specs, out_specs=out_specs, check_vma=False)
```

profile of v0, /device:TPU:5, one launch (start us, length us, event | category | flops | bytes accessed | tf_op | source)
XLA Modules:
  0.0 452.8 jit_solution(945619041920369671)
XLA Ops:
  6.5 4.7 %fusion.28 = f32[1024,576]{0,1:T(8,128)} fusion(bf16[1024,896]{1,0:T(8,128)(2,1)} %param.13, bf16[896,2112]{0,1:T(8,128)(2,1)} %param.19), kind=kOutput, calls=%fused_computation.27 | convolution fusion | flops 1056964608 | bytes 5226496 | tf_op jit(solution)/shard_map/dot_general | solution.py:61
  11.3 1.9 fusion.65
  13.3 0.6 copy-done.11
  14.0 66.2 %all-reduce.3.cloned.1.call-done = (f32[1024,576]{0,1:T(8,128)}, f32[2,16,2112]{2,1,0:T(8,128)}) async-done(((f32[1024,576]{0,1:T(8,128)}, f32[2,16,2112]{2,1,0:T(8,128)}), (f32[1024,576]{0,1:T(8,128)}, f32[2,16,2112]{2,1,0:T(8,128)})) %all-reduce.3.cloned.1.call-update) | async-done | bytes 2629648 | tf_op jit(solution)/shard_map/psum | solution.py:67
  80.2 1.9 multiply_reduce_fusion
  82.1 1.5 fusion.38
  83.7 0.2 multiply_convert_fusion
  83.9 1.1 pad_maximum_fusion
  85.1 26.7 %copy.47 = bf16[16,1024,576]{2,1,0:T(8,128)(2,1)} copy(bf16[16,1024,576]{1,2,0:T(8,128)(2,1)} %param.16) | data formatting | bytes 37748736 | tf_op jit(solution)/shard_map/reshape | solution.py:81
  112.0 12.8 %copy.33 = bf16[1536,3072]{0,1:T(8,128)(2,1)} copy(bf16[1536,3072]{1,0:T(8,128)(2,1)} %param.22) | data formatting | bytes 18874368 | tf_op args[9]
  124.8 20.0 %all_gather.13 = s32[16384]{0:T(1024)S(1)} all-gather(s32[1024]{0:T(1024)S(1)} %copy-done.8), channel_id=1, replica_groups=mesh['seq'=16,'head'=8] {'seq'}, dimensions={0}, use_global_device_ids=true | all-gather | bytes 69632 | tf_op jit(solution)/shard_map/all_gather | solution.py:75
  144.8 20.3 %all_gather.12 = s32[16384,1]{0,1:T(1,128)S(1)} all-gather(s32[1024,1]{0,1:T(1,128)S(1)} %copy-done.10), channel_id=1, replica_groups=mesh['seq'=16,'head'=8] {'seq'}, dimensions={0}, use_global_device_ids=true | all-gather | bytes 69632 | tf_op jit(solution)/shard_map/all_gather | solution.py:74
  165.2 0.2 compare_reduce_fusion
  165.4 0.1 iota_compare_fusion
  165.8 0.1 multiply_cosine_fusion.1
  166.0 6.9 %fusion.43 = f32[2,16,16,192]{3,1,2,0:T(8,128)S(1)} fusion(bf16[16,192,1536,1]{2,1,0,3:T(8,128)(2,1)} %bitcast.79, f32[2,16,2112]{2,1,0:T(8,128)S(1)} %copy-done.6, f32[1536]{0:T(1024)S(1)} %convert_element_type.54, f32[2,16]{1,0:T(2,128)S(1)} %add_rsqrt_fusion.1), kind=kOutput, calls=%fused_computation.54 | convolution fusion | flops 302137344 | bytes 10036224 | tf_op jit(solution)/shard_map/dot_general | solution.py:86
  172.9 0.2 subtract_convert_fusion
  173.1 0.4 fusion.15
  173.5 0.1 pad_maximum_fusion.1
  173.6 37.5 %all-gather.3.cloned.1.call-done = bf16[16384,576]{0,1:T(8,128)(2,1)} async-done(((bf16[1024,576]{0,1:T(8,128)(2,1)}), bf16[16384,576]{0,1:T(8,128)(2,1)}) %all-gather.3.cloned.1.call-update) | async-done | bytes 18874384 | tf_op jit(solution)/shard_map/all_gather | solution.py:73
  211.1 26.5 %copy.30 = bf16[16384,576]{1,0:T(8,128)(2,1)} copy(bf16[16384,576]{0,1:T(8,128)(2,1)} %all-gather.3.cloned.1.call-done) | data formatting | bytes 37748736 | tf_op jit(solution)/shard_map/all_gather | solution.py:73
  237.6 89.7 %scatter_fusion = bf16[16384,576]{1,0:T(8,128)(2,1)} fusion(bf16[16384,576]{1,0:T(8,128)(2,1)} %bitcast.76, s32[16384]{0:T(1024)S(1)} %compare_select_fusion, bf16[16384,576]{1,0:T(8,128)(2,1)} %copy.30), kind=kCustom, calls=%fused_computation | custom fusion | bytes 56688640 | tf_op jit(solution)/shard_map/scatter | solution.py:82
  327.3 19.6 %scatter_custom_fusion.1 = bf16[16384,576]{1,0:T(8,128)(2,1)} fusion(bf16[16384,576]{1,0:T(8,128)(2,1)} %scatter_fusion, s32[32]{0:T(128)S(1)} %fusion.57, bf16[32,32]{1,0:T(8,128)(2,1)S(1)} %bitcast.84, bf16[]{:T(256)} %constant.52, bf16[32,32]{1,0:T(8,128)(2,1)S(1)} %bitcast.85, bf16[32,512]{1,0:T(8,128)(2,1)S(1)} %bitcast.82), kind=kCustom, calls=%fused_computation.59 | custom fusion | flops 110592 | bytes 18924032 | tf_op jit(solution)/shard_map/scatter | solution.py:83
  346.9 10.4 %fusion.30 = f32[16,1024,2,16]{1,3,2,0:T(8,128)S(1)} fusion(bf16[16,1024,576,1]{2,1,3,0:T(8,128)(2,1)} %bitcast.77, bf16[2,16,16,576]{3,1,0,2:T(8,128)(2,1)S(1)} %pad_maximum_fusion.1), kind=kOutput, calls=%fused_computation.30 | convolution fusion | flops 603979776 | bytes 21561344 | tf_op jit(solution)/shard_map/srhc,rlc->srhl/dot_general | solution.py:96
  357.3 1.3 copy-done.4
  358.7 0.7 fusion.64
  359.4 9.4 %fusion.14 = bf16[2,16,16,576]{3,2,0,1:T(8,128)(2,1)S(1)} fusion(bf16[16,1024,576,1]{2,1,3,0:T(8,128)(2,1)} %bitcast.78, f32[2,16,16]{2,0,1:T(2,128)S(1)} %fusion.64, f32[16,1024,2,16]{1,3,2,0:T(8,128)} %copy-done.4, pred[2,16,1024]{2,0,1:T(4,128)(4,1)S(1)} %iota_compare_fusion), kind=kOutput, calls=%fused_computation.18 | convolution fusion | flops 606897664 | bytes 21596160 | tf_op jit(solution)/shard_map/srhl,rlc->srhc/dot_general | solution.py:106
  368.8 0.6 fusion.21
  369.5 0.7 copy.68
  370.2 44.0 %all-gather.5.cloned.1.call-done = bf16[2,256,2048]{2,1,0:T(8,128)(2,1)} async-done(((bf16[2,16,2048]{2,1,0:T(8,128)(2,1)}), bf16[2,256,2048]{2,1,0:T(8,128)(2,1)}) %all-gather.5.cloned.1.call-update) | async-done | bytes 2097168 | tf_op jit(solution)/shard_map/all_gather | solution.py:114
  414.2 4.3 fusion.8
  418.6 27.3 %reduce-scatter.2.cloned.1.call-done = bf16[2,32,448]{2,1,0:T(8,128)(2,1)} async-done(((bf16[2,256,448]{2,1,0:T(8,128)(2,1)}), bf16[2,32,448]{2,1,0:T(8,128)(2,1)}) %reduce-scatter.2.cloned.1.call-update) | async-done | bytes 57360 | tf_op jit(solution)/shard_map/reduce_scatter | solution.py:118
  (49 shorter events, 0.8 us)
Async XLA Ops:
  6.5 166.6 %copy-start = (bf16[16,128,512]{2,1,0:T(8,128)(2,1)S(1)}, bf16[16,128,512]{2,1,0:T(8,128)(2,1)}, u32[]{:S(2)}) copy-start(bf16[16,128,512]{2,1,0:T(8,128)(2,1)} %param.23) | copy-start | bytes 6291460
  6.5 4.8 %copy-start.7 = (bf16[2,16,896]{2,1,0:T(8,128)(2,1)S(1)}, bf16[2,16,896]{2,1,0:T(8,128)(2,1)}, u32[]{:S(2)}) copy-start(bf16[2,16,896]{2,1,0:T(8,128)(2,1)} %param.18) | copy-start | bytes 172036
  6.5 73.7 %all-reduce.3.cloned.1.call-start = ((), (), s32[]{:S(2)}) async-start(), calls=%async_computation.4 | async-start | bytes 5275648 | tf_op jit(solution)/shard_map/psum | solution.py:67
  6.5 4.7 %copy-start.3 = (bf16[896,2112]{0,1:T(8,128)(2,1)S(1)}, bf16[896,2112]{0,1:T(8,128)(2,1)}, u32[]{:S(2)}) copy-start(bf16[896,2112]{0,1:T(8,128)(2,1)} %param.19) | copy-start | bytes 11354116
  13.2 0.7 copy-start.11
  13.2 0.7 copy-start.8
  13.3 197.8 %all-gather.3.cloned.1.call-start = ((), (), s32[]{:S(2)}) async-start(), calls=%async_computation.1 | async-start | bytes 20054016 | tf_op jit(solution)/shard_map/all_gather | solution.py:73
  80.2 3.5 copy-start.2
  85.0 329.1 %all-gather.5.cloned.1.call-start = ((), (), s32[]{:S(2)}) async-start(), calls=%async_computation.2 | async-start | bytes 2228224 | tf_op jit(solution)/shard_map/all_gather | solution.py:114
  85.1 26.8 %copy-start.12 = (s32[16]{0:T(128)S(1)}, s32[16]{0:T(128)}, u32[]{:S(2)}) copy-start(s32[16]{0:T(128)} %param.17) | copy-start | bytes 196
  112.0 12.8 %copy-start.9 = (bf16[1536]{0:T(1024)(128)(2,1)S(1)}, bf16[1536]{0:T(1024)(128)(2,1)}, u32[]{:S(2)}) copy-start(bf16[1536]{0:T(1024)(128)(2,1)} %param.20) | copy-start | bytes 9220
  112.0 32.9 %copy-start.10 = (s32[1024,1]{0,1:T(1,128)S(1)}, s32[1024,1]{0,1:T(1,128)}, u32[]{:S(2)}) copy-start(s32[1024,1]{0,1:T(1,128)} %param.14) | copy-start | bytes 12292
  112.0 53.6 %copy-start.6 = (f32[2,16,2112]{2,1,0:T(8,128)S(1)}, f32[2,16,2112]{2,1,0:T(8,128)}, u32[]{:S(2)}) copy-start(f32[2,16,2112]{2,1,0:T(8,128)} %get-tuple-element.6) | copy-start | bytes 811012
  357.3 1.4 copy-start.4
  359.4 9.4 %copy-start.5 = (bf16[16,512,128]{2,1,0:T(8,128)(2,1)S(1)}, bf16[16,512,128]{2,1,0:T(8,128)(2,1)}, u32[]{:S(2)}) copy-start(bf16[16,512,128]{2,1,0:T(8,128)(2,1)} %param.24) | copy-start | bytes 6291460
  370.2 75.7 %reduce-scatter.2.cloned.1.call-start = ((), (), s32[]{:S(2)}) async-start(), calls=%async_computation.3 | async-start | bytes 589824 | tf_op jit(solution)/shard_map/reduce_scatter | solution.py:118
  414.2 31.7 %copy-start.1 = (bf16[16,128,512]{2,1,0:T(8,128)(2,1)S(1)}, bf16[16,128,512]{2,1,0:T(8,128)(2,1)}, u32[]{:S(2)}) copy-start(bf16[16,128,512]{2,1,0:T(8,128)(2,1)} %param.23) | copy-start | bytes 6291460
Sparse Core Ops, SparseCore 0:
  13.4 66.7 all-reduce.2
  85.2 125.8 all-gather.2
  370.3 43.8 all-gather.4
  418.7 27.1 reduce-scatter.1
where the time goes:
time: 462 us; the launch traced here: 453 us
  waiting for transfers between devices  175 us (38%)
  local copies, waits for them, and re-layouts  159 us (34%)
  blocking collectives  40.4 us (9%)
  matrix products  38.7 us (8%)
  other arithmetic  26.2 us (6%)
  between operations  13.8 us (3%)
    scatter x1, local copies, waits for them, and re-layouts, local(): flat = flat.at[got_targets].set(all_rows, mode='drop')  89.7 us
    psum x1, waiting for transfers between devices, local(): prompt_part, new_part = lax.psum((prompt_part, new_part), 'head')  66.2 us
    all_gather x1, waiting for transfers between devices, local(): lax.all_gather(heads_out, 'seq', axis=1, tiled=True)  44 us
    all_gather x1, waiting for transfers between devices, local(): lax.all_gather(prompt_rows, 'seq', axis=0, tiled=True)  37.5 us
    reduce_scatter x1, waiting for transfers between devices, local(): lax.psum_scatter(terms.astype(jnp.bfloat16), 'head', scatter_dimension=1,...  27.3 us
    reshape x1, local copies, waits for them, and re-layouts, local(): flat = cache.reshape(limit, width)  26.7 us
    all_gather x1, local copies, waits for them, and re-layouts, local(): lax.all_gather(prompt_rows, 'seq', axis=0, tiled=True)  26.5 us
    all_gather x1, blocking collectives, local(): lax.all_gather(owner, 'seq', axis=0, tiled=True)  20.3 us
  transfers between devices with their start and end apart: 4, of which 4 were waited for; matrix products, arithmetic and copies ran while one was open for 11% of the time, Pallas kernels for 0%

commit v1 on v0

v1 whole, which is shorter than its diff:
```python
import functools

import jax
import jax.numpy as jnp
from jax import lax
from jax.experimental import pallas as pl
from jax.experimental.pallas import tpu as pltpu
from jax.sharding import PartitionSpec as P

F32 = jnp.float32
BF16 = jnp.bfloat16
I32 = jnp.int32
MESH = pl.DeviceIdType.MESH
QRANK = 1536
LATENT = 512
ROPE = 64
NOPE = 128
VDIM = 128
HIDE = -1e30
LOG2E = 1.4426950408889634


def nt(a, b):
    return lax.dot_general(a, b, (((1,), (1,)), ((), ())), preferred_element_type=F32)


def nn(a, b):
    return jnp.dot(a, b, preferred_element_type=F32)


def iota(shape, dim):
    return lax.broadcasted_iota(I32, shape, dim)


def one_hot(cond):
    return jnp.where(cond, 1.0, 0.0).astype(BF16)


def kernel(
    own_r, off_r, ctab, ex, ntab, nex, qex, vis, wrow, gq, gkv, newh,
    hid_h, wd_h, uq_h, uk_h, cache_h, uv_h, wo_h,
    out,
    hid, wd, uq, uk, kc, uv, wo, lsem, ksem,
    rs, tsend, trecv, ts_sem, tr_sem,
    npp, npair, npx, npxr, npfin, np_ss, np_rs,
    wr, part, ps, pr, xs, xr, mine, p_ss, p_rs, x_ss, x_rs,
    disp, slots, d_ss, d_rs, g_ss, g_rs,
    qls, ql, qs, newk, biasm, acc, m_s, l_s, ob, op,
    hog, h_ss, h_rs, osend, orecv, o_ss, o_rs,
):
    i = lax.axis_index("seq")
    j = lax.axis_index("head")
    x = j // 2
    c = j % 2
    z = i // 4
    y = i % 4
    sib = 2 * x + (1 - c)

    def load(src, dst, sem):
        cp = pltpu.make_async_copy(src, dst, sem)
        cp.start()
        return cp

    def remote(src, dst, ss, rr, dev):
        return pltpu.make_async_remote_copy(
            src_ref=src, dst_ref=dst, send_sem=ss, recv_sem=rr,
            device_id=dev, device_id_type=MESH,
        )

    c_wd = load(wd_h, wd, lsem.at[0])
    c_hid = load(hid_h, hid, lsem.at[1])

    barrier = pltpu.get_barrier_semaphore()
    for dj in range(1, 8):
        pl.semaphore_signal(barrier, inc=1, device_id=(i, (j + dj) % 8), device_id_type=MESH)
    for di in range(1, 16):
        pl.semaphore_signal(barrier, inc=1, device_id=((i + di) % 16, j), device_id_type=MESH)

    sub128 = iota((128, 128), 0)
    lane128 = iota((128, 128), 1)
    upper = one_hot(sub128 < lane128)
    sub16 = iota((16, 128), 0)
    hots, pres = [], []
    count = jnp.zeros((16, 1), F32)
    for b in range(8):
        hot = jnp.where(sub16 == own_r[b : b + 1, :], 1.0, 0.0)
        pres.append(nn(hot.astype(BF16), upper) + count)
        hots.append(hot)
        count = count + jnp.sum(hot, axis=1, keepdims=True)
    count = jnp.broadcast_to(count, (16, 128))
    start = jnp.zeros((16, 128), F32)
    for o in range(15):
        start = start + jnp.where(sub16 > o, count[o : o + 1, :], 0.0)
    table = jnp.zeros((48, 128), F32)
    for b in range(8):
        place = jnp.sum(hots[b] * (pres[b] + start), axis=0, keepdims=True).astype(I32)
        dev = place & 7
        at = place >> 3
        rs[b : b + 1, :] = dev * 128 + at
        key = dev * 16 + (at & 15)
        off = off_r[b : b + 1, :]
        high = (off >> 7).astype(F32)
        low = (off & 127).astype(F32)
        digits = jnp.concatenate([hots[b] * high, hots[b] * low, hots[b]], axis=0).astype(BF16)
        table = table + nt(digits, one_hot(sub128 == key))
    cells = jnp.where(table[32:48] > 0.5, table[0:16] * 128.0 + table[16:32], -1.0)
    for o in range(16):
        tsend[o] = jnp.broadcast_to(cells[o : o + 1, :], (8, 128))
    row_place = (iota((16, 128), 1) * 8 + j).astype(F32)
    owner_at = jnp.sum(
        jnp.where(row_place >= start + count, 1.0, 0.0), axis=0, keepdims=True
    ).astype(I32)
    slot_at = owner_at * 16 + (iota((1, 128), 1) & 15)
    rs[8:9, :] = slot_at

    pl.semaphore_wait(barrier, 22)

    def t_copy(di):
        to = (i + di) % 16
        return remote(tsend.at[to], trecv.at[i], ts_sem.at[di], tr_sem.at[di], (to, j))

    for di in range(1, 16):
        t_copy(di).start()

    c_wd.wait()
    c_uq = load(uq_h, uq, lsem.at[2])
    c_uk = load(uk_h, uk, lsem.at[3])
    wr[0:64, :] = wd[2048:2112, :]
    wr[64:96, :] = wd[2080:2112, :]
    wr[96:128, :] = wd[2048:2080, :]
    npp[0] = nt(newh[...], wd[0:1152, :]).astype(BF16)
    npp[1, :, 0:896] = nt(newh[...], wd[1152:2048, :]).astype(BF16)
    npp[1, :, 896:1024] = nt(newh[...], wr[...]).astype(BF16)
    npp[1, :, 1024:1152] = jnp.zeros((32, 128), BF16)
    np_pair = remote(npp.at[1 - c], npair, np_ss.at[0], np_rs.at[0], (i, sib))
    np_pair.start()

    c_hid.wait()

    def k_copy(r):
        return pltpu.make_async_copy(cache_h.at[r], kc.at[r], ksem.at[r])

    @pl.loop(0, 16)
    def _(r):
        k_copy(r).start()

    c_uv = load(uv_h, uv, lsem.at[4])
    c_wo = load(wo_h, wo, lsem.at[5])
    low_lane = iota((256, 128), 1) < 64

    @pl.loop(0, 4)
    def _(t):
        rows = pl.ds(pl.multiple_of(t * 256, 256), 256)
        h = hid[rows, :]
        part[rows, 0:512] = nt(h, wd[1536:2048, :]).astype(BF16)
        u = nt(h, wr[...]) * ctab[rows, :]
        u = u + pltpu.roll(u, 64, 1)
        part[rows, 512:640] = jnp.where(low_lane, u, ex[rows, :].astype(F32)).astype(BF16)

    def permuted(first, second):
        ids = rs[0:8, :]
        top = [one_hot(sub128 == ids[b : b + 1, :] - first * 128) for b in range(8)]
        low = [one_hot(sub128 == ids[b : b + 1, :] - second * 128) for b in range(8)]
        pick = jnp.concatenate(
            [jnp.concatenate(top, axis=1), jnp.concatenate(low, axis=1)], axis=0
        )
        return nn(pick, part[...])

    def p_copy(dx):
        return remote(ps.at[dx], pr.at[dx], p_ss.at[dx], p_rs.at[dx], (i, sib))

    for first, second in ((2, 1), (3, 0)):
        both = permuted(2 * ((x + first) % 4) + 1 - c, 2 * ((x + second) % 4) + 1 - c)
        ps[first] = both[0:128].astype(BF16)
        ps[second] = both[128:256].astype(BF16)
        p_copy(first).start()
        p_copy(second).start()

    np_pair.wait_recv()
    npx[...] = (npp[c].astype(F32) + npair[...].astype(F32)).astype(BF16)

    def npx_copy(dx):
        return remote(
            npx, npxr.at[dx], np_ss.at[dx], np_rs.at[dx], (i, 2 * ((x + dx) % 4) + c)
        )

    for dx in (2, 1, 3):
        npx_copy(dx).start()

    def x_copy(dx):
        return remote(
            xs.at[dx], xr.at[dx], x_ss.at[dx], x_rs.at[dx], (i, 2 * ((x + dx) % 4) + c)
        )

    for first, second in ((2, 1), (3, 0)):
        both = permuted(2 * ((x + first) % 4) + c, 2 * ((x + second) % 4) + c)
        p_copy(first).wait_recv()
        xs[first] = (both[0:128] + pr[first].astype(F32)).astype(BF16)
        x_copy(first).start()
        p_copy(second).wait_recv()
        if second == 0:
            mine[...] = both[128:256] + pr[0].astype(F32)
        else:
            xs[second] = (both[128:256] + pr[second].astype(F32)).astype(BF16)
            x_copy(second).start()

    total = npx[...].astype(F32)
    for dx in (1, 3, 2):
        npx_copy(dx).wait_recv()
        total = total + npxr[dx].astype(F32)
    npfin[c] = total.astype(BF16)
    np_swap = remote(npfin.at[c], npfin.at[c], np_ss.at[4], np_rs.at[4], (i, sib))
    np_swap.start()
    np_swap_in = remote(npfin.at[1 - c], npfin.at[1 - c], np_ss.at[4], np_rs.at[4], (i, sib))
    np_swap_in.wait_recv()

    low32 = iota((32, 128), 1) < 64
    q_in = jnp.concatenate([npfin[0], npfin[1, :, 0:384]], axis=1).astype(F32)
    q_in = q_in * lax.rsqrt(jnp.mean(q_in * q_in, axis=1, keepdims=True) + 1e-6) * gq[...]
    qls[...] = q_in.astype(BF16)
    k_in = npfin[1, :, 384:896].astype(F32)
    k_in = k_in * lax.rsqrt(jnp.mean(k_in * k_in, axis=1, keepdims=True) + 1e-6) * gkv[...]
    newk[0:32, 0:512] = k_in.astype(BF16)
    newk[32:128, 0:512] = jnp.zeros((96, 512), BF16)
    u = npfin[1, :, 896:1024].astype(F32) * ntab[0]
    u = u + pltpu.roll(u, 64, 1)
    newk[0:32, 512:640] = jnp.where(low32, u, nex[0:32, :]).astype(BF16)
    newk[32:128, 512:640] = nex[32:128, :].astype(BF16)

    c_uq.wait()
    c_uk.wait()
    inner = (iota((32, 128), 1) & 63) < 32

    @pl.loop(0, 8)
    def _(p):
        q = nn(qls[...], uq[:, pl.ds(pl.multiple_of(p * 384, 384), 384)])
        t0, t1, t2 = q[:, 0:128], q[:, 128:256], q[:, 256:384]
        odd = jnp.where(low32, pltpu.roll(t1, 64, 1), pltpu.roll(t2, 64, 1))
        rope = jnp.where(low32, t1, t2)
        turned = jnp.where(inner, pltpu.roll(rope, 96, 1), pltpu.roll(rope, 32, 1))
        rope = rope * ntab[1] + turned * ntab[2]
        for s, (nope, rot) in enumerate(((t0, rope), (odd, pltpu.roll(rope, 64, 1)))):
            rows = pl.ds(pl.multiple_of(p * 64 + s * 32, 32), 32)
            ql[rows, 0:512] = nn(nope.astype(BF16), uk[2 * p + s]).astype(BF16)
            ql[rows, 512:640] = jnp.where(low32, rot, qex[...]).astype(BF16)

    @pl.loop(0, 2)
    def _(t):
        n = iota((256, 512), 0) + t * 256
        want = ((n & 31) >> 1) * 32 + (n & 1) * 16 + (n >> 5)
        rows = pl.ds(pl.multiple_of(t * 256, 256), 256)
        qs[rows, :] = nn(one_hot(iota((256, 512), 1) == want), ql[...]).astype(BF16)

    total = mine[...]
    for dx in (1, 3, 2):
        x_copy(dx).wait_recv()
        total = total + xr[dx].astype(F32)
    lat = total[:, 0:512]
    lat = lat * lax.rsqrt(jnp.mean(lat * lat, axis=1, keepdims=True) + 1e-6) * gkv[...]
    tail = total[:, 512:640]
    tail = jnp.where(iota((128, 128), 1) < 64, tail, tail * 0.125)
    rows_b = jnp.concatenate([lat, tail], axis=1).astype(BF16)
    spread = one_hot(iota((256, 128), 0) == rs[8:9, :])
    disp[...] = nn(spread, rows_b).astype(BF16)

    def d_copy(di):
        to = (i + di) % 16
        return remote(
            disp.at[pl.ds(pl.multiple_of(to * 16, 16), 16), :],
            slots.at[j, pl.ds(pl.multiple_of(i * 16, 16), 16), :],
            d_ss.at[di], d_rs.at[di], (to, j),
        )

    for di in range(1, 16):
        d_copy(di).start()
    at_me = pl.ds(pl.multiple_of(i * 16, 16), 16)
    slots[j, at_me, :] = disp[at_me, :]

    at_src = tsend[i]
    trecv[i] = at_src
    for di in range(1, 16):
        src = (i + 16 - di) % 16
        remote(tsend.at[src], trecv.at[src], ts_sem.at[di], tr_sem.at[di], (src, j)).wait_recv()

    def add_cells(s, total):
        cell = trecv[s, 0:1, :].astype(I32)
        return total + nt(one_hot(sub128 == (cell >> 7)), one_hot(sub128 == (cell & 127)))

    taken = lax.fori_loop(0, 16, add_cells, jnp.zeros((128, 128), F32))
    biasm[...] = jnp.where((taken < 0.5) & (vis[...] > 0.5), 0.0, HIDE)

    unit = LOG2E / (NOPE + ROPE) ** 0.5

    def cache_part(r):
        k_copy(r).wait()
        rows = pl.ds(pl.multiple_of(r * 32, 32), 32)
        s = nn(qs[rows, 0:576], kc[r])
        b8 = biasm[pl.ds(pl.multiple_of(r * 8, 8), 8), :]
        s = s + jnp.concatenate([b8[g : g + 1, :] for g in range(8)], axis=1)
        sn = nt(qs[rows, :], newk[...])
        m = jnp.maximum(jnp.max(s, axis=1, keepdims=True), jnp.max(sn, axis=1, keepdims=True))
        e = jnp.exp2((s - m) * unit)
        en = jnp.exp2((sn - m) * unit)
        l = jnp.sum(e, axis=1, keepdims=True) + jnp.sum(en, axis=1, keepdims=True)
        acc[rows, :] = nt(e.astype(BF16), kc[r, 0:512, :]) + nn(en.astype(BF16), newk[:, 0:512])
        m_s[rows, :] = jnp.broadcast_to(m, (32, 128))
        l_s[rows, :] = jnp.broadcast_to(l, (32, 128))

    @pl.loop(0, 6)
    def _(r):
        cache_part(r)

    for di in range(1, 16):
        src = (i + 16 - di) % 16
        remote(
            disp.at[pl.ds(pl.multiple_of(src * 16, 16), 16), :],
            slots.at[j, pl.ds(pl.multiple_of(src * 16, 16), 16), :],
            d_ss.at[di], d_rs.at[di], (src, j),
        ).wait_recv()
    marks = slots[j, :, 512:640].astype(F32)
    left = jnp.sum(marks * wrow[0:1, :], axis=1, keepdims=True)
    marks = jnp.where(
        iota((256, 128), 1) == 80, jnp.where(left > 0.5, 0.0, 1.0), marks
    )
    slots[j, :, 512:640] = marks.astype(BF16)

    def g_copy(dx):
        return remote(
            slots.at[j], slots.at[j], g_ss.at[dx], g_rs.at[j], (i, 2 * ((x + dx) % 4) + c)
        )

    def g_sib(block, k):
        return remote(slots.at[block], slots.at[block], g_ss.at[k], g_rs.at[block], (i, sib))

    for dx in (2, 1, 3):
        g_copy(dx).start()
    g_sib(j, 0).start()

    @pl.loop(6, 16)
    def _(r):
        cache_part(r)

    def slot_part(block):
        @pl.loop(0, 2)
        def _(t):
            rows = pl.ds(pl.multiple_of(t * 256, 256), 256)
            s = nt(qs[rows, :], slots[block])
            old = m_s[rows, 0:1]
            m = jnp.maximum(old, jnp.max(s, axis=1, keepdims=True))
            keep = jnp.exp2((old - m) * unit)
            e = jnp.exp2((s - m) * unit)
            l_s[rows, :] = l_s[rows, :] * keep + jnp.sum(e, axis=1, keepdims=True)
            acc[rows, :] = acc[rows, :] * keep + nn(e.astype(BF16), slots[block, :, 0:512])
            m_s[rows, :] = jnp.broadcast_to(m, (256, 128))

    def g_wait(block):
        remote(slots.at[block], slots.at[block], g_ss.at[0], g_rs.at[block], (i, sib)).wait_recv()

    slot_part(j)
    g_wait(sib)
    slot_part(sib)
    for k, dx in enumerate((1, 3, 2)):
        block = 2 * ((x + dx) % 4) + c
        g_wait(block)
        g_sib(block, 4 + k).start()
        slot_part(block)
    for dx in (1, 3, 2):
        block = 2 * ((x + dx) % 4) + 1 - c
        g_wait(block)
        slot_part(block)

    @pl.loop(0, 2)
    def _(t):
        rows = pl.ds(pl.multiple_of(t * 256, 256), 256)
        ob[rows, :] = (acc[rows, :] * (1.0 / l_s[rows, 0:1])).astype(BF16)

    @pl.loop(0, 2)
    def _(t):
        n = iota((256, 512), 0) + t * 256
        want = (n & 15) * 32 + (n >> 5) * 2 + ((n >> 4) & 1)
        rows = pl.ds(pl.multiple_of(t * 256, 256), 256)
        op[rows, :] = nn(one_hot(iota((256, 512), 1) == want), ob[...]).astype(BF16)

    c_uv.wait()
    c_wo.wait()

    def o_dev(dz, dy):
        return ((z + dz) % 4) * 4 + (y + dy) % 4

    def h_copy(half, piece, k, to):
        return remote(
            hog.at[half, piece], hog.at[half, piece], h_ss.at[half, k], h_rs.at[half, piece],
            (to, j),
        )

    def h_wait(half, piece):
        remote(
            hog.at[half, piece], hog.at[half, piece], h_ss.at[half, 0], h_rs.at[half, piece],
            (i, sib),
        ).wait_recv()

    def near(half, d):
        return o_dev(0, d) if half == 0 else o_dev(d, 0)

    def far(half, d):
        return o_dev(d, 0) if half == 0 else o_dev(0, d)

    sent = []
    for half in range(2):
        for h in range(8):
            hog[half, i, :, h * 128 : (h + 1) * 128] = nn(
                op[(half * 8 + h) * 32 : (half * 8 + h + 1) * 32, :], uv[half * 8 + h]
            ).astype(BF16)
        for k, d in enumerate((2, 1, 3)):
            cp = h_copy(half, i, k, near(half, d))
            cp.start()
            sent.append(cp)
        for k, d in enumerate((2, 1, 3)):
            cp = h_copy(half, i, 3 + k, far(half, d))
            cp.start()
            sent.append(cp)
    for q, e in enumerate((1, 3, 2)):
        for half in range(2):
            piece = near(half, e)
            h_wait(half, piece)
            for k, d in enumerate((2, 1, 3)):
                cp = h_copy(half, piece, 6 + 3 * q + k, far(half, d))
                cp.start()
                sent.append(cp)

    def o_copy(to):
        return remote(osend.at[to], orecv.at[j], o_ss.at[to], o_rs.at[j], (i, to))

    for dz in (0, 1, 3, 2):
        row = (z + dz) % 4
        for dy in range(4):
            piece = o_dev(dz, dy)
            if dz != 0:
                h_wait(0, piece)
            if dy != 0:
                h_wait(1, piece)
        four = pl.ds(row * 4, 4)
        res = nt(hog[0, four].reshape(128, 1024), wo[:, 0:1024])
        res = res + nt(hog[1, four].reshape(128, 1024), wo[:, 1024:2048])
        for k in range(2):
            to = row * 2 + k
            osend[to, :, 0:448] = res[k * 64 : (k + 1) * 64, :].astype(BF16)

            @pl.when(to != j)
            def _():
                o_copy(to).start()

    total = osend[j, :, 0:448].astype(F32)
    for dj in range(1, 8):
        src = (j + dj) % 8
        remote(osend.at[src], orecv.at[src], o_ss.at[src], o_rs.at[src], (i, src)).wait_recv()
        total = total + orecv[src, :, 0:448].astype(F32)
    total = total.astype(BF16)
    for o in range(2):
        for s in range(2):
            out[s, o * 16 : (o + 1) * 16, :] = total[o * 32 + s * 16 : o * 32 + s * 16 + 16, :]

    for di in range(1, 16):
        t_copy(di).wait_send()
        d_copy(di).wait_send()
    np_pair.wait_send()
    np_swap.wait_send()
    for dx in range(4):
        p_copy(dx).wait_send()
    for dx in range(1, 4):
        npx_copy(dx).wait_send()
        x_copy(dx).wait_send()
        g_copy(dx).wait_send()
    g_sib(j, 0).wait_send()
    for k, dx in enumerate((1, 3, 2)):
        g_sib(2 * ((x + dx) % 4) + c, 4 + k).wait_send()
    for cp in sent:
        cp.wait_send()
    for dj in range(1, 8):
        o_copy((j + dj) % 8).wait_send()


def local(
    prompt_hidden, owner, offsets, cache, lengths, new_hidden, w_down,
    gain_q, gain_kv, w_uq, w_uk, w_uv, w_out,
):
    half = ROPE // 2
    inverse = 10000.0 ** (-jnp.arange(half, dtype=F32) / half)
    angles = (offsets % 1024).astype(F32)[:, None] * inverse
    cos, sin = jnp.cos(angles), jnp.sin(angles)
    ctab = jnp.concatenate([cos, cos, -sin, sin], axis=1)
    lane = jnp.arange(128, dtype=I32)[None, :]
    off = offsets[:, None]
    place = off % 1024
    ex = (
        jnp.where(lane == 64 + off // 1024, 1, 0)
        + jnp.where(lane == 81, place // 128, 0)
        + jnp.where(lane == 82, place % 128, 0)
    ).astype(BF16)
    positions = (lengths[None, :] + jnp.arange(2, dtype=I32)[:, None]).reshape(32)
    angles = positions.astype(F32)[:, None] * inverse
    cos, sin = jnp.cos(angles), jnp.sin(angles)
    ntab = jnp.stack(
        [
            jnp.concatenate([cos, cos, -sin, sin], axis=1),
            jnp.concatenate([cos, cos, cos, cos], axis=1),
            jnp.concatenate([-sin, sin, -sin, sin], axis=1),
        ]
    )
    row = jnp.arange(128, dtype=I32)[:, None]
    nex = jnp.where(
        row < 32,
        jnp.where(lane == 64 + row % 16, 1.0, 0.0) + jnp.where(lane == 83, row // 16, 0),
        jnp.where(lane == 80, 1.0, 0.0),
    ).astype(F32)
    row = row[:32]
    other = (lane >= 64) & (lane < 80) & (lane != 64 + row % 16)
    qex = jnp.where(other | (lane == 80) | ((lane == 83) & (row < 16)), HIDE, 0.0).astype(F32)
    cell = jnp.arange(16384, dtype=I32).reshape(16, 1024)
    vis = jnp.where((cell % 1024) < lengths[:, None], 1.0, 0.0).astype(F32).reshape(128, 128)
    wrow = jnp.concatenate(
        [jnp.zeros((64,), F32), lengths.astype(F32), jnp.array([0.0, -128.0, -1.0], F32),
         jnp.zeros((45,), F32)]
    )
    wrow = jnp.broadcast_to(wrow[None, :], (8, 128))

    vm = pl.BlockSpec(memory_space=pltpu.VMEM)
    hb = pl.BlockSpec(memory_space=pl.ANY)
    V = pltpu.VMEM
    S = pltpu.SemaphoreType.DMA
    scratch = [
        V((1024, 896), BF16), V((2112, 896), BF16), V((1536, 3072), BF16), V((16, 128, 512), BF16),
        V((16, 576, 1024), BF16), V((16, 512, 128), BF16), V((448, 2048), BF16), S((6,)), S((16,)),
        V((16, 128), I32), V((16, 8, 128), F32), V((16, 8, 128), F32), S((16,)), S((16,)),
        V((2, 32, 1152), BF16), V((32, 1152), BF16), V((32, 1152), BF16), V((4, 32, 1152), BF16),
        V((2, 32, 1152), BF16), S((5,)), S((5,)),
        V((128, 896), BF16), V((1024, 640), BF16), V((4, 128, 640), BF16), V((4, 128, 640), BF16),
        V((4, 128, 640), BF16), V((4, 128, 640), BF16), V((128, 640), F32),
        S((4,)), S((4,)), S((4,)), S((4,)),
        V((256, 640), BF16), V((8, 256, 640), BF16), S((16,)), S((16,)), S((8,)), S((8,)),
        V((32, 1536), BF16), V((512, 640), BF16), V((512, 640), BF16), V((128, 640), BF16),
        V((128, 128), F32), V((512, 512), F32), V((512, 128), F32), V((512, 128), F32),
        V((512, 512), BF16), V((512, 512), BF16),
        V((2, 16, 32, 1024), BF16), S((2, 15)), S((2, 16)),
        V((8, 64, 512), BF16), V((8, 64, 512), BF16), S((8,)), S((8,)),
    ]
    return pl.pallas_call(
        kernel,
        out_shape=jax.ShapeDtypeStruct((2, 32, 448), BF16),
        in_specs=[vm] * 12 + [hb] * 7,
        out_specs=vm,
        scratch_shapes=scratch,
        compiler_params=pltpu.CompilerParams(
            collective_id=0, has_side_effects=True, vmem_limit_bytes=60 * 1024 * 1024
        ),
    )(
        owner.reshape(8, 128), offsets.reshape(8, 128), ctab, ex, ntab, nex, qex, vis, wrow,
        gain_q.astype(F32).reshape(1, QRANK), gain_kv.astype(F32).reshape(1, LATENT),
        new_hidden.reshape(32, 896),
        prompt_hidden, w_down.T, w_uq, w_uk, jnp.swapaxes(cache, 1, 2), w_uv, w_out.T,
    )


def solution(mesh):
    in_specs = (
        P("seq", "head"), P("seq", None), P("seq"), P("seq", None, None), P("seq"),
        P(None, "seq", "head"), P("head", None), P(), P(), P(None, "head"),
        P("head", None, None), P("head", None, None), P("head", "seq"),
    )
    return jax.shard_map(
        local, mesh=mesh, in_specs=in_specs, out_specs=P(None, "head", "seq"), check_vma=False
    )
```

time: 462 us -> 102 us (0.22); the launches traced: 453 us -> 102 us
  waiting for transfers between devices: 175 us -> 0 us
  local copies, waits for them, and re-layouts: 159 us -> 3.02 us
  Pallas kernels: 0 us -> 89.5 us
  blocking collectives: 40.4 us -> 0 us
  matrix products: 38.7 us -> 0 us
  other arithmetic: 26.2 us -> 9.01 us
  between operations: 13.8 us -> 0.1 us
    scatter x1 -> x0, local copies, waits for them, and re-layouts: 89.7 us -> none  [local(): flat = flat.at[got_targets].set(all_rows, mode='drop')]
    pallas_call x0 -> x1, Pallas kernels: none -> 89.5 us  [local(): pl.pallas_call(kernel, out_shape=jax.ShapeDtypeStruct((2, 32, 448), BF16)...]
    all_gather x2 -> x0, waiting for transfers between devices: 81.4 us -> none  [the longest x1 44 us: local(): lax.all_gather(heads_out, 'seq', axis=1, tiled=True)]
    psum x1 -> x0, waiting for transfers between devices: 66.2 us -> none  [local(): prompt_part, new_part = lax.psum((prompt_part, new_part), 'head')]
    all_gather x2 -> x0, blocking collectives: 40.4 us -> none  [the longest x1 20.3 us: local(): lax.all_gather(owner, 'seq', axis=0, tiled=True)]
    dot_general x8 -> x0, matrix products: 38.7 us -> none  [the longest x1 10.4 us: local(): jnp.einsum('srhc,rlc->srhl', joined, keys, preferred_element_type=jnp.flo...]
    reduce_scatter x1 -> x0, waiting for transfers between devices: 27.3 us -> none  [local(): lax.psum_scatter(terms.astype(jnp.bfloat16), 'head', scatter_dimension=1,...]
    reshape x2, local copies, waits for them, and re-layouts: 27.4 us -> 0.68 us  [the longest x1 0.6 us: local(): gain_q.astype(F32).reshape(1, QRANK)]
  transfers between devices with their start and end apart: 4 -> 0, of which waited for: 4 -> 0; matrix products, arithmetic and copies ran while one was open for 11% -> 0% of each run, Pallas kernels for 0% -> 0%
where the time goes in v1:
time: 102 us
  Pallas kernels  89.5 us (88%)
  other arithmetic  9.01 us (9%)
  local copies, waits for them, and re-layouts  3.02 us (3%)
    pallas_call x1, Pallas kernels, local(): pl.pallas_call(kernel, out_shape=jax.ShapeDtypeStruct((2, 32, 448), BF16)...  89.5 us
    cos x2, other arithmetic, local(): cos, sin = (jnp.cos(angles), jnp.sin(angles))  2.04 us

profile of v1, /device:TPU:5, one launch (start us, length us, event | category | flops | bytes accessed | tf_op | source)
XLA Modules:
  0.0 101.6 jit_solution(8722051470764783406)
XLA Ops:
  0.0 0.0 copy-start.2
  0.0 0.7 fusion.12
  0.7 0.0 copy-start.3
  0.7 0.0 copy-start
  0.8 0.0 copy-start.1
  0.8 1.9 %multiply_cosine_fusion = (f32[1024,32]{1,0:T(8,128)S(1)}, f32[1024,32]{1,0:T(8,128)S(1)}, f32[1024,32]{1,0:T(8,128)S(1)}) fusion(f32[1024]{0:T(1024)S(1)} %get-tuple-element.14, f32[32]{0:T(128)S(1)} %multiply_power_fusion), kind=kLoop, calls=%fused_computation.1 | loop fusion | flops 65536 | bytes 397440 | tf_op jit(solution)/shard_map/cos | solution.py:490
  2.7 1.3 %pad_maximum_fusion.ctab = f32[1024,128]{1,0:T(8,128)} fusion(f32[1024,32]{1,0:T(8,128)S(1)} %get-tuple-element.10, f32[1024,32]{1,0:T(8,128)S(1)} %get-tuple-element.9, f32[1024,32]{1,0:T(8,128)S(1)} %get-tuple-element.8), kind=kLoop, calls=%fused_computation.2 | loop fusion | flops 393216 | bytes 917504 | tf_op jit(solution)/shard_map/concatenate | solution.py:491
  4.0 1.4 %add_convert_fusion.ex = bf16[1024,128]{1,0:T(8,128)(2,1)} fusion(s32[1024]{0:T(1024)S(1)} %get-tuple-element.13, s32[1024]{0:T(1024)S(1)} %get-tuple-element.12, s32[1024]{0:T(1024)S(1)} %get-tuple-element.11, pred[128]{0:T(512)(128)(4,1)S(1)} %get-tuple-element.18, pred[128]{0:T(512)(128)(4,1)S(1)} %get-tuple-element.19), kind=kLoop, calls=%fused_computation.3 | loop fusion | flops 917504 | bytes 274688 | tf_op jit(solution)/shard_map/convert_element_type | solution.py:499
  5.3 0.0 copy-done.2
  5.3 0.1 convert_element_type.27
  5.4 0.1 multiply_cosine_fusion.1
  5.6 0.1 maximum_bitcast_fusion
  5.7 0.6 pad_maximum_fusion.1.ntab
  6.3 0.8 add_select_fusion.1.nex
  7.1 0.7 fusion.10.qex
  7.8 0.1 lt.77
  7.9 0.1 lt.78
  8.0 0.1 reshape.209
  8.1 0.7 fusion.5.vis
  8.8 0.0 copy-done.3
  8.8 0.1 pad_maximum_fusion.3
  8.9 0.6 broadcast_in_dim.142.wrow
  9.5 0.0 copy-done
  9.5 0.6 reshape.217.gq
  10.1 0.0 copy-done.1
  10.1 0.6 reshape.218
  10.6 89.5 %shard_map.136 = bf16[2,32,448]{2,1,0:T(8,128)(2,1)} custom-call(s32[8,128]{1,0:T(8,128)} %bitcast.41, s32[8,128]{1,0:T(8,128)} %bitcast.39, f32[1024,128]{1,0:T(8,128)} %pad_maximum_fusion.ctab, bf16[1024,128]{1,0:T(8,128)(2,1)} %add_convert_fusion.ex, f32[3,32,128]{2,1,0:T(8,128)} %pad_maximum_fusion.1.ntab, f32[128,128]{1,0:T(8,128)} %add_select_fusion.1.nex, ...), custom_call_target="tpu_custom_call" | custom-call | tf_op jit(solution)/shard_map/pallas_call | solution.py:547
  100.1 1.5 %copy.17 = bf16[2,32,448]{2,1,0:T(8,128)(2,1)} copy(bf16[2,32,448]{2,1,0:T(8,128)(2,1)} %shard_map.136) | data formatting | bytes 114688
  (15 shorter events, 0.1 us)
Async XLA Ops:
  0.0 5.3 %copy-start.2 = (s32[16]{0:T(128)S(1)}, s32[16]{0:T(128)}, u32[]{:S(2)}) copy-start(s32[16]{0:T(128)} %param.18) | copy-start | bytes 196
  0.7 8.1 %copy-start.3 = (f32[3]{0:T(128)S(1)}, f32[3]{0:T(128)}, u32[]{:S(2)}) copy-start(f32[3]{0:T(128)} %constant.133.clone) | copy-start | bytes 40
  0.7 8.7 %copy-start = (bf16[1536]{0:T(1024)(128)(2,1)S(1)}, bf16[1536]{0:T(1024)(128)(2,1)}, u32[]{:S(2)}) copy-start(bf16[1536]{0:T(1024)(128)(2,1)} %param.21) | copy-start | bytes 9220
  0.8 9.3 %copy-start.1 = (bf16[512]{0:T(512)(128)(2,1)S(1)}, bf16[512]{0:T(512)(128)(2,1)}, u32[]{:S(2)}) copy-start(bf16[512]{0:T(512)(128)(2,1)} %param.22) | copy-start | bytes 3076

commit v2 on v1

v2 whole, which is shorter than its diff:
```python
import functools

import jax
import jax.numpy as jnp
from jax import lax
from jax.experimental import pallas as pl
from jax.experimental.pallas import tpu as pltpu
from jax.sharding import PartitionSpec as P

F32 = jnp.float32
BF16 = jnp.bfloat16
I32 = jnp.int32
MESH = pl.DeviceIdType.MESH
QRANK = 1536
LATENT = 512
ROPE = 64
NOPE = 128
VDIM = 128
HIDE = -1e30
LOG2E = 1.4426950408889634
LOG2_BASE = 13.287712379549449


def nt(a, b):
    return lax.dot_general(a, b, (((1,), (1,)), ((), ())), preferred_element_type=F32)


def nn(a, b):
    return jnp.dot(a, b, preferred_element_type=F32)


def iota(shape, dim):
    return lax.broadcasted_iota(I32, shape, dim)


def one_hot(cond):
    return jnp.where(cond, 1.0, 0.0).astype(BF16)


def turn_rate(lane):
    return jnp.exp2((lane & 31).astype(F32) * (-LOG2_BASE / (ROPE // 2)))


def turned(v):
    inner = (iota(v.shape, 1) & 63) < 32
    return jnp.where(inner, pltpu.roll(v, 96, 1), pltpu.roll(v, 32, 1))


def kernel(
    lens, own_r, off_r, gain_q, gain_kv, newh,
    hid_h, wd_h, uq_h, uk_h, cache_h, uv_h, wo_h,
    out,
    hid, wd, uq, uk, kc, uv, wo, lsem, ksem,
    rs, feat, tsend, trecv, ts_sem, tr_sem,
    npp, npair, npx, npxr, npfin, np_ss, np_rs, ntab,
    part, ps, pr, xs, xr, mine, p_ss, p_rs, x_ss, x_rs,
    disp, slots, d_ss, d_rs, g_ss, g_rs,
    qls, ql, qs, newk, biasm, acc, m_s, l_s, ob, op,
    hog, h_ss, h_rs, ores, opair, opin, op_ss, op_rs, osend, orecv, o_ss, o_rs,
):
    i = lax.axis_index("seq")
    j = lax.axis_index("head")
    x = j // 2
    c = j % 2
    z = i // 4
    y = i % 4
    sib = 2 * x + (1 - c)

    def load(src, dst, sem):
        cp = pltpu.make_async_copy(src, dst, sem)
        cp.start()
        return cp

    def remote(src, dst, ss, rr, dev):
        return pltpu.make_async_remote_copy(
            src_ref=src, dst_ref=dst, send_sem=ss, recv_sem=rr,
            device_id=dev, device_id_type=MESH,
        )

    barrier = pltpu.get_barrier_semaphore()
    for dj in range(1, 8):
        pl.semaphore_signal(barrier, inc=1, device_id=(i, (j + dj) % 8), device_id_type=MESH)
    for di in range(1, 16):
        pl.semaphore_signal(barrier, inc=1, device_id=((i + di) % 16, j), device_id_type=MESH)

    c_wd = load(wd_h, wd, lsem.at[0])
    c_hid = load(hid_h, hid, lsem.at[1])

    sub128 = iota((128, 128), 0)
    lane128 = iota((128, 128), 1)
    sub16 = iota((16, 128), 0)
    hot = jnp.concatenate(
        [jnp.where(sub16 == own_r[b : b + 1, :], 1.0, 0.0) for b in range(8)], axis=0
    )
    hot_b = hot.astype(BF16)
    ahead = nn(hot_b, one_hot(sub128 < lane128))
    count = nn(hot_b, jnp.ones((128, 128), BF16)).astype(BF16)
    before = ((lane128 & 15) < (sub128 & 15)) | (
        ((lane128 & 15) == (sub128 & 15)) & ((lane128 >> 4) < (sub128 >> 4))
    )
    ahead = ahead + nn(one_hot(before), count)
    ends = nn(one_hot((iota((16, 128), 1) & 15) <= sub16), count)
    place = jnp.sum((hot * ahead).reshape(8, 16, 128), axis=1).astype(I32)
    dev = place & 7
    at = place >> 3
    rs[0:8, :] = dev * 128 + at
    key = dev * 16 + (at & 15)
    mine_at = rs[0:8, :] - j * 128
    off = off_r[...]
    digits, keys, marks, picks = [], [], [], []
    sub32 = iota((32, 128), 0)
    for b in range(8):
        one = slice(b, b + 1)
        high, low = (off[one] >> 7).astype(F32), (off[one] & 127).astype(F32)
        hb = hot[b * 16 : b * 16 + 16]
        digits.append(jnp.concatenate([hb * high, hb * low, hb], axis=0).astype(BF16))
        keys.append(one_hot(sub128 == key[one]))
        mark = jnp.where(sub32 == (off[one] >> 10), 1.0, 0.0)
        mark = jnp.where(sub32 == 17, ((off[one] >> 7) & 7).astype(F32), mark)
        mark = jnp.where(sub32 == 18, low, mark)
        marks.append(
            jnp.concatenate([jnp.zeros((64, 128), F32), mark, jnp.zeros((32, 128), F32)], axis=0)
            .astype(BF16)
        )
        picks.append(one_hot(sub128 == mine_at[one]))
    table = nt(jnp.concatenate(digits, axis=1), jnp.concatenate(keys, axis=1))
    feat[...] = nt(jnp.concatenate(picks, axis=1), jnp.concatenate(marks, axis=1))
    cells = jnp.where(table[32:48] > 0.5, table[0:16] * 128.0 + table[16:32], -1.0)
    for o in range(16):
        tsend[o] = jnp.broadcast_to(cells[o : o + 1, :], (8, 128))
    row_place = (iota((16, 128), 1) * 8 + j).astype(F32)
    owner_at = jnp.sum(
        jnp.where(row_place >= ends, 1.0, 0.0), axis=0, keepdims=True
    ).astype(I32)
    slot_at = owner_at * 16 + (iota((1, 128), 1) & 15)
    rs[8:9, :] = slot_at
    request = iota((32, 128), 0) & 15
    position = iota((32, 128), 0) >> 4
    for r in range(16):
        position = position + jnp.where(request == r, lens[r], 0)
    lane32 = iota((32, 128), 1)
    angle = position.astype(F32) * turn_rate(lane32)
    ntab[0] = jnp.cos(angle)
    ntab[1] = jnp.where((lane32 & 63) < 32, -1.0, 1.0) * jnp.sin(angle)

    c_wd.wait()
    c_uq = load(uq_h, uq, lsem.at[2])
    c_uk = load(uk_h, uk, lsem.at[3])
    npp[0] = nt(newh[...], wd[0:1152, :]).astype(BF16)
    npp[1, :, 0:896] = nt(newh[...], wd[1152:2048, :]).astype(BF16)
    tail = nt(newh[...], wd[2048:2112, :])
    npp[1, :, 896:1024] = jnp.concatenate([tail, tail], axis=1).astype(BF16)
    npp[1, :, 1024:1152] = jnp.zeros((32, 128), BF16)
    c_hid.wait()

    def k_copy(r):
        return pltpu.make_async_copy(cache_h.at[r], kc.at[r], ksem.at[r])

    @pl.loop(0, 16)
    def _(r):
        k_copy(r).start()

    c_uv = load(uv_h, uv, lsem.at[4])
    c_wo = load(wo_h, wo, lsem.at[5])
    def project(t):
        rows = pl.ds(t * 512, 512)
        h = hid[rows, :]
        part[rows, 0:512] = nt(h, wd[1536:2048, :]).astype(BF16)
        u = nt(h, wd[2048:2112, :])
        part[rows, 512:640] = jnp.concatenate([u, u], axis=1).astype(BF16)

    def npx_copy(dx):
        return remote(
            npx, npxr.at[dx], np_ss.at[dx], np_rs.at[dx], (i, 2 * ((x + dx) % 4) + c)
        )

    project(0)
    project(1)

    def permuted(first, second):
        ids = rs[0:8, :]
        top = [one_hot(sub128 == ids[b : b + 1, :] - first * 128) for b in range(8)]
        low = [one_hot(sub128 == ids[b : b + 1, :] - second * 128) for b in range(8)]
        pick = jnp.concatenate(
            [jnp.concatenate(top, axis=1), jnp.concatenate(low, axis=1)], axis=0
        )
        return nn(pick, part[...])

    def p_copy(dx):
        return remote(ps.at[dx], pr.at[dx], p_ss.at[dx], p_rs.at[dx], (i, sib))

    def via_copy(k):
        return remote(
            xs.at[2, pl.ds(64 * k, 64), :], xr.at[2, pl.ds(64 * k, 64), :],
            x_ss.at[k], x_rs.at[k], (i, 2 * ((x + 1 + 2 * k) % 4) + c),
        )

    def x_copy(dx, k):
        rows = pl.ds(64 * k, 64)
        return remote(
            xs.at[dx, rows, :], xr.at[dx, rows, :], x_ss.at[2 * dx + k], x_rs.at[2 * dx + k],
            (i, 2 * ((x + dx) % 4) + c),
        )

    for first, second in ((2, 1), (3, 0)):
        both = permuted(2 * ((x + first) % 4) + 1 - c, 2 * ((x + second) % 4) + 1 - c)
        ps[first] = both[0:128].astype(BF16)
        ps[second] = both[128:256].astype(BF16)

    pl.semaphore_wait(barrier, 22)
    np_pair = remote(npp.at[1 - c], npair, np_ss.at[0], np_rs.at[0], (i, sib))
    np_pair.start()
    for dx in (2, 1, 3, 0):
        p_copy(dx).start()

    def t_copy(di):
        to = (i + di) % 16
        return remote(tsend.at[to], trecv.at[i], ts_sem.at[di], tr_sem.at[di], (to, j))

    for di in range(1, 16):
        t_copy(di).start()
    both = permuted(2 * ((x + 2) % 4) + c, 2 * ((x + 1) % 4) + c)
    np_pair.wait_recv()
    npx[...] = (npp[c].astype(F32) + npair[...].astype(F32)).astype(BF16)
    for dx in (2, 1, 3):
        npx_copy(dx).start()
    p_copy(2).wait_recv()
    xs[2] = (both[0:128] + pr[2].astype(F32)).astype(BF16)
    via_copy(0).start()
    via_copy(1).start()
    p_copy(1).wait_recv()
    up = both[128:256] + pr[1].astype(F32)
    xs[1, 64:128, :] = up[64:128].astype(BF16)
    x_copy(1, 1).start()
    both = permuted(2 * ((x + 3) % 4) + c, 2 * x + c)
    p_copy(3).wait_recv()
    down = both[0:128] + pr[3].astype(F32)
    xs[3, 0:64, :] = down[0:64].astype(BF16)
    x_copy(3, 0).start()
    p_copy(0).wait_recv()
    mine[...] = both[128:256] + pr[0].astype(F32)

    total = npx[...].astype(F32)
    for dx in (1, 3, 2):
        npx_copy(dx).wait_recv()
        total = total + npxr[dx].astype(F32)
    npfin[c] = total.astype(BF16)
    np_swap = remote(npfin.at[c], npfin.at[c], np_ss.at[4], np_rs.at[4], (i, sib))
    np_swap.start()
    via_copy(0).wait_recv()
    xs[1, 0:64, :] = (up[0:64] + xr[2, 0:64, :].astype(F32)).astype(BF16)
    x_copy(1, 0).start()
    via_copy(1).wait_recv()
    xs[3, 64:128, :] = (down[64:128] + xr[2, 64:128, :].astype(F32)).astype(BF16)
    x_copy(3, 1).start()
    np_swap_in = remote(npfin.at[1 - c], npfin.at[1 - c], np_ss.at[4], np_rs.at[4], (i, sib))
    np_swap_in.wait_recv()

    unit = LOG2E / (NOPE + ROPE) ** 0.5
    low32 = iota((32, 128), 1) < 64
    q_in = jnp.concatenate([npfin[0], npfin[1, :, 0:384]], axis=1).astype(F32)
    q_in = q_in * lax.rsqrt(jnp.mean(q_in * q_in, axis=1, keepdims=True) + 1e-6) * gain_q[...].astype(F32).reshape(1, QRANK)
    qls[...] = q_in.astype(BF16)
    k_in = npfin[1, :, 384:896].astype(F32)
    k_in = k_in * lax.rsqrt(jnp.mean(k_in * k_in, axis=1, keepdims=True) + 1e-6) * gain_kv[...].astype(F32).reshape(1, LATENT)
    newk[0:32, 0:512] = k_in.astype(BF16)
    newk[32:128, 0:512] = jnp.zeros((96, 512), BF16)
    u = npfin[1, :, 896:1024].astype(F32)
    u = u * ntab[0] + turned(u) * ntab[1]
    row32 = iota((32, 128), 0)
    own_lane = lane32 == 64 + (row32 & 15)
    late = (lane32 == 83) & (row32 >= 16)
    u = jnp.where(low32, u, jnp.where(own_lane | late, 1.0, 0.0))
    newk[0:32, 512:640] = u.astype(BF16)
    newk[32:128, 512:640] = one_hot(iota((96, 128), 1) == 80)
    other = (lane32 >= 64) & (lane32 < 81) & jnp.logical_not(own_lane)
    qex = jnp.where(other | ((lane32 == 83) & (row32 < 16)), HIDE, 0.0)

    c_uq.wait()
    c_uk.wait()

    def two_heads(p):
        q = nn(qls[...], uq[:, pl.ds(pl.multiple_of(p * 384, 384), 384)])
        t0, t1, t2 = q[:, 0:128], q[:, 128:256], q[:, 256:384]
        odd = jnp.where(low32, pltpu.roll(t1, 64, 1), pltpu.roll(t2, 64, 1))
        rope = jnp.where(low32, t1, t2)
        rope = rope * ntab[0] + turned(rope) * ntab[1]
        for s, (nope, rot) in enumerate(((t0, rope), (odd, pltpu.roll(rope, 64, 1)))):
            rows = pl.ds(pl.multiple_of(p * 64 + s * 32, 32), 32)
            ql[rows, 0:512] = (nn(nope.astype(BF16), uk[2 * p + s]) * unit).astype(BF16)
            ql[rows, 512:640] = jnp.where(low32, rot * unit, qex).astype(BF16)

    @pl.loop(0, 4)
    def _(p):
        two_heads(2 * p)
        two_heads(2 * p + 1)

    @pl.loop(0, 2)
    def _(t):
        n = iota((256, 512), 0) + t * 256
        want = ((n & 31) >> 1) * 32 + (n & 1) * 16 + (n >> 5)
        rows = pl.ds(pl.multiple_of(t * 256, 256), 256)
        qs[rows, :] = nn(one_hot(iota((256, 512), 1) == want), ql[...]).astype(BF16)

    total = mine[...]
    for dx in (1, 3):
        x_copy(dx, 0).wait_recv()
        x_copy(dx, 1).wait_recv()
        total = total + xr[dx].astype(F32)
    lat = total[:, 0:512]
    lat = lat * lax.rsqrt(jnp.mean(lat * lat, axis=1, keepdims=True) + 1e-6) * gain_kv[...].astype(F32).reshape(1, LATENT)
    tail = total[:, 512:640]
    marks = feat[...]
    at = jnp.where(lane128 == 81, 128.0, jnp.where(lane128 == 82, 1.0, 0.0))
    at = jnp.sum(marks * at, axis=1, keepdims=True)
    angle = at * turn_rate(lane128)
    sign = jnp.where((lane128 & 63) < 32, -1.0, 1.0)
    tail = tail * jnp.cos(angle) + turned(tail) * (sign * jnp.sin(angle))
    tail = jnp.where(lane128 < 64, tail, marks)
    rows_b = jnp.concatenate([lat, tail], axis=1).astype(BF16)
    spread = one_hot(iota((256, 128), 0) == rs[8:9, :])
    disp[...] = nn(spread, rows_b).astype(BF16)

    def d_copy(di):
        to = (i + di) % 16
        return remote(
            disp.at[pl.ds(pl.multiple_of(to * 16, 16), 16), :],
            slots.at[j, pl.ds(pl.multiple_of(i * 16, 16), 16), :],
            d_ss.at[di], d_rs.at[di], (to, j),
        )

    for di in range(1, 16):
        d_copy(di).start()
    at_me = pl.ds(pl.multiple_of(i * 16, 16), 16)
    slots[j, at_me, :] = disp[at_me, :]

    at_src = tsend[i]
    trecv[i] = at_src
    for di in range(1, 16):
        src = (i + 16 - di) % 16
        remote(tsend.at[src], trecv.at[src], ts_sem.at[di], tr_sem.at[di], (src, j)).wait_recv()

    tall, wide = [], []
    for s in range(16):
        cell = trecv[s, 0:1, :].astype(I32)
        tall.append(one_hot(sub128 == (cell >> 7)))
        wide.append(one_hot(sub128 == (cell & 127)))
    taken = nt(jnp.concatenate(tall, axis=1), jnp.concatenate(wide, axis=1))
    length = jnp.zeros((128, 128), I32)
    weigh = jnp.where(iota((8, 128), 1) == 81, -128.0, 0.0)
    weigh = jnp.where(iota((8, 128), 1) == 82, -1.0, weigh)
    for r in range(16):
        length = length + jnp.where((sub128 >> 3) == r, lens[r], 0)
        weigh = weigh + jnp.where(iota((8, 128), 1) == 64 + r, lens[r], 0).astype(F32)
    seen = (sub128 & 7) * 128 + lane128 < length
    biasm[...] = jnp.where((taken < 0.5) & seen, 0.0, HIDE)

    def cache_part(r):
        rows = pl.ds(pl.multiple_of(r * 32, 32), 32)
        s = nn(qs[rows, 0:576], kc[r])
        b8 = biasm[pl.ds(pl.multiple_of(r * 8, 8), 8), :]
        s = [s[:, g * 128 : (g + 1) * 128] + b8[g : g + 1, :] for g in range(8)]
        s.append(nt(qs[rows, :], newk[...]))
        top = jnp.max(functools.reduce(jnp.maximum, s), axis=1, keepdims=True)
        m = jnp.broadcast_to(top, (32, 128))
        e = [jnp.exp2(v - m) for v in s]
        m_s[rows, :] = m
        l_s[rows, :] = functools.reduce(jnp.add, e)
        e = [v.astype(BF16) for v in e]
        acc[rows, :] = nt(jnp.concatenate(e[0:8], axis=1), kc[r, 0:512, :]) + nn(
            e[8], newk[:, 0:512]
        )

    def cache_four(t):
        for r in range(4):
            k_copy(4 * t + r).wait()
        for r in range(4):
            cache_part(4 * t + r)

    @pl.loop(0, 1)
    def _(t):
        cache_four(t)

    for di in range(1, 16):
        src = (i + 16 - di) % 16
        remote(
            disp.at[pl.ds(pl.multiple_of(src * 16, 16), 16), :],
            slots.at[j, pl.ds(pl.multiple_of(src * 16, 16), 16), :],
            d_ss.at[di], d_rs.at[di], (src, j),
        ).wait_recv()
    marks = slots[j, :, 512:640].astype(F32)
    left = jnp.sum(marks * weigh[0:1, :], axis=1, keepdims=True)
    marks = jnp.where(
        iota((256, 128), 1) == 80, jnp.where(left > 0.5, 0.0, 1.0), marks
    )
    slots[j, :, 512:640] = marks.astype(BF16)

    def g_half(block, k):
        return slots.at[block, pl.ds(128 * k, 128), :]

    def g_copy(block, k, ss, to):
        return remote(
            g_half(block, k), g_half(block, k), g_ss.at[ss], g_rs.at[block, k], (i, to)
        )

    def g_wait(block, k):
        g_copy(block, k, 0, sib).wait_recv()

    above, below, across = 2 * ((x + 1) % 4), 2 * ((x + 3) % 4), 2 * ((x + 2) % 4)
    g_sent = []

    def g_send(block, k, to):
        cp = g_copy(block, k, len(g_sent), to)
        cp.start()
        g_sent.append(cp)

    g_send(j, 0, above + c)
    g_send(j, 1, below + c)
    g_send(j, 1, above + c)
    g_send(j, 0, below + c)
    g_send(j, 0, sib)
    g_send(j, 1, sib)

    def slot_part(first, second):
        q = qs[...]
        blocks = (first, second)
        s = [nt(q, slots[b]) for b in blocks]
        s = [v[:, g * 128 : (g + 1) * 128] for v in s for g in range(2)]
        old = m_s[...]
        top = jnp.max(functools.reduce(jnp.maximum, s), axis=1, keepdims=True)
        m = jnp.maximum(old, jnp.broadcast_to(top, (512, 128)))
        keep = jnp.exp2(old - m)
        e = [jnp.exp2(v - m) for v in s]
        m_s[...] = m
        l_s[...] = l_s[...] * keep + functools.reduce(jnp.add, e)
        e = [v.astype(BF16) for v in e]
        val = nn(jnp.concatenate(e[0:2], axis=1), slots[first, :, 0:512])
        val = val + nn(jnp.concatenate(e[2:4], axis=1), slots[second, :, 0:512])
        acc[...] = acc[...] * jnp.concatenate([keep] * 4, axis=1) + val

    @pl.loop(1, 2)
    def _(t):
        cache_four(t)

    g_wait(below + c, 0)
    g_send(below + c, 0, above + c)
    g_wait(above + c, 1)
    g_send(above + c, 1, below + c)
    g_send(below + c, 0, sib)
    g_send(above + c, 1, sib)

    @pl.loop(2, 3)
    def _(t):
        cache_four(t)

    g_wait(below + c, 1)
    g_send(below + c, 1, sib)
    g_wait(above + c, 0)
    g_send(above + c, 0, sib)

    @pl.loop(3, 4)
    def _(t):
        cache_four(t)

    @pl.loop(0, 2)
    def _(t):
        chip = 2 * ((x + 3 * t) % 4)
        for k in range(2):
            g_wait(chip + 1 - c, k)
        slot_part(chip + c, chip + 1 - c)

    g_wait(across + c, 0)
    g_send(across + c, 0, sib)
    g_wait(across + c, 1)
    g_send(across + c, 1, sib)

    @pl.loop(0, 2)
    def _(t):
        chip = 2 * ((x + 1 + t) % 4)
        for k in range(2):
            g_wait(chip + 1 - c, k)
        slot_part(chip + c, chip + 1 - c)

    @pl.loop(0, 2)
    def _(t):
        rows = pl.ds(pl.multiple_of(t * 256, 256), 256)
        ob[rows, :] = (
            acc[rows, :] * (1.0 / jnp.sum(l_s[rows, :], axis=1, keepdims=True))
        ).astype(BF16)

    @pl.loop(0, 2)
    def _(t):
        n = iota((256, 512), 0) + t * 256
        want = (n & 15) * 32 + (n >> 5) * 2 + ((n >> 4) & 1)
        rows = pl.ds(pl.multiple_of(t * 256, 256), 256)
        op[rows, :] = nn(one_hot(iota((256, 512), 1) == want), ob[...]).astype(BF16)

    c_uv.wait()
    c_wo.wait()

    def o_dev(dz, dy):
        return ((z + dz) % 4) * 4 + (y + dy) % 4

    def near(half, d):
        return o_dev(0, d) if half == 0 else o_dev(d, 0)

    def far(half, d):
        return o_dev(d, 0) if half == 0 else o_dev(0, d)

    def cross(half, n, f):
        return o_dev(f, n) if half == 0 else o_dev(n, f)

    h_sent = []

    def h_copy(half, piece, part_at, k, to):
        ref = hog.at[half, piece]
        if part_at is not None:
            ref = hog.at[half, piece, pl.ds(16 * part_at, 16), :]
        return remote(ref, ref, h_ss.at[k], h_rs.at[half, piece, part_at or 0], (to, j))

    def h_send(half, piece, part_at, to):
        cp = h_copy(half, piece, part_at, len(h_sent), to)
        cp.start()
        h_sent.append(cp)

    def h_wait(half, piece, part_at=None):
        h_copy(half, piece, part_at, 0, i).wait_recv()

    halves = range(2)
    for half in halves:
        for h in range(8):
            hog[half, i, :, h * 128 : (h + 1) * 128] = nn(
                op[(half * 8 + h) * 32 : (half * 8 + h + 1) * 32, :], uv[half * 8 + h]
            ).astype(BF16)
        for d in (1, 3):
            h_send(half, i, None, near(half, d))
        for d in (1, 3):
            h_send(half, i, None, far(half, d))

    def pass_on(half, n, f, to):
        piece = cross(half, n, f)
        h_wait(half, piece)
        h_send(half, piece, 0 if (f == 3 or (f == 0 and n == 3)) else 1, to)

    for n in (3, 1):
        for half in halves:
            pass_on(half, n, 0, near(half, 4 - n))
            for d in (1, 3):
                h_send(half, near(half, n), None, far(half, d))
    for f in (3, 1):
        for half in halves:
            pass_on(half, 0, f, far(half, 4 - f))
    for half in halves:
        h_wait(half, near(half, 2), 0)
        h_wait(half, near(half, 2), 1)
        for d in (1, 3):
            h_send(half, near(half, 2), None, far(half, d))
    for n in (3, 1):
        for f in (3, 1):
            for half in halves:
                pass_on(half, n, f, far(half, 4 - f))

    def o_pair(t):
        return remote(opair.at[t], opin.at[t], op_ss.at[t], op_rs.at[t], (i, sib))

    def o_copy(t, to):
        return remote(osend.at[t], orecv.at[x], o_ss.at[t], o_rs.at[x], (i, 2 * to + c))

    def columns(t, row):
        four = pl.ds(row * 4, 4)
        res = nt(hog[0, four].reshape(128, 1024), wo[:, 0:1024])
        res = res + nt(hog[1, four].reshape(128, 1024), wo[:, 1024:2048])
        ores[t, :, 0:448] = res
        opair[t, :, 0:448] = ores[t, pl.ds(pl.multiple_of((1 - c) * 64, 64), 64), 0:448].astype(
            BF16
        )
        o_pair(t).start()

    def onward(t, row):
        o_pair(t).wait_recv()
        own_half = ores[t, pl.ds(pl.multiple_of(c * 64, 64), 64), :]
        osend[t] = (own_half + opin[t].astype(F32)).astype(BF16)

        @pl.when(row != x)
        def _():
            o_copy(t, row).start()

        @pl.when(row == x)
        def _():
            orecv[x] = osend[t]

    order = (0, 3, 1, 2)
    rows_at = [(z + dz) % 4 for dz in order]
    h_wait(1, far(1, 2), 0)
    h_wait(1, far(1, 2), 1)
    columns(0, rows_at[0])
    for t, d in ((1, 3), (2, 1)):
        h_wait(0, cross(0, 2, d))
        h_send(0, cross(0, 2, d), 0 if d == 3 else 1, far(0, 4 - d))
        h_wait(1, cross(1, 2, d))
        h_send(1, cross(1, 2, d), 0 if d == 3 else 1, far(1, 4 - d))
        for k in range(2):
            h_wait(1, cross(1, d, 2), k)
        columns(t, rows_at[t])
        onward(t - 1, rows_at[t - 1])
    for n in range(4):
        for k in range(2):
            h_wait(0, cross(0, n, 2), k)
    for k in range(2):
        h_wait(1, cross(1, 2, 2), k)
    columns(3, rows_at[3])
    onward(2, rows_at[2])
    onward(3, rows_at[3])

    total = jnp.zeros((64, 448), F32)
    for dx in range(1, 4):
        src = (x + dx) % 4
        remote(osend.at[0], orecv.at[src], o_ss.at[0], o_rs.at[src], (i, 2 * src + c)).wait_recv()
    for src in range(4):
        total = total + orecv[src, :, 0:448].astype(F32)
    total = total.astype(BF16)
    for o in range(2):
        for s in range(2):
            out[s, o * 16 : (o + 1) * 16, :] = total[o * 32 + s * 16 : o * 32 + s * 16 + 16, :]

    for di in range(1, 16):
        t_copy(di).wait_send()
        d_copy(di).wait_send()
    np_pair.wait_send()
    np_swap.wait_send()
    for dx in range(4):
        p_copy(dx).wait_send()
    for dx in range(1, 4):
        npx_copy(dx).wait_send()
    for k in range(2):
        x_copy(1, k).wait_send()
        x_copy(3, k).wait_send()
        via_copy(k).wait_send()
    for cp in g_sent + h_sent:
        cp.wait_send()
    for t in range(4):
        o_pair(t).wait_send()

        @pl.when(rows_at[t] != x)
        def _():
            o_copy(t, rows_at[t]).wait_send()


def local(
    prompt_hidden, owner, offsets, cache, lengths, new_hidden, w_down,
    gain_q, gain_kv, w_uq, w_uk, w_uv, w_out,
):
    vm = pl.BlockSpec(memory_space=pltpu.VMEM)
    hb = pl.BlockSpec(memory_space=pl.ANY)
    V = pltpu.VMEM
    S = pltpu.SemaphoreType.DMA
    scratch = [
        V((1024, 896), BF16), V((2112, 896), BF16), V((1536, 3072), BF16), V((16, 128, 512), BF16),
        V((16, 576, 1024), BF16), V((16, 512, 128), BF16), V((448, 2048), BF16), S((6,)), S((16,)),
        V((16, 128), I32), V((128, 128), F32), V((16, 8, 128), F32), V((16, 8, 128), F32), S((16,)), S((16,)),
        V((2, 32, 1152), BF16), V((32, 1152), BF16), V((32, 1152), BF16), V((4, 32, 1152), BF16),
        V((2, 32, 1152), BF16), S((5,)), S((5,)), V((2, 32, 128), F32),
        V((1024, 640), BF16), V((4, 128, 640), BF16), V((4, 128, 640), BF16),
        V((4, 128, 640), BF16), V((4, 128, 640), BF16), V((128, 640), F32),
        S((4,)), S((4,)), S((8,)), S((8,)),
        V((256, 640), BF16), V((8, 256, 640), BF16), S((16,)), S((16,)), S((14,)), S((8, 2)),
        V((32, 1536), BF16), V((512, 640), BF16), V((512, 640), BF16), V((128, 640), BF16),
        V((128, 128), F32), V((512, 512), F32), V((512, 128), F32), V((512, 128), F32),
        V((512, 512), BF16), V((512, 512), BF16),
        V((2, 16, 32, 1024), BF16), S((40,)), S((2, 16, 2)),
        V((4, 128, 512), F32), V((4, 64, 512), BF16), V((4, 64, 512), BF16), S((4,)), S((4,)),
        V((4, 64, 512), BF16), V((4, 64, 512), BF16), S((4,)), S((4,)),
    ]
    return pl.pallas_call(
        kernel,
        out_shape=jax.ShapeDtypeStruct((2, 32, 448), BF16),
        in_specs=[pl.BlockSpec(memory_space=pltpu.SMEM)] + [vm] * 5 + [hb] * 7,
        out_specs=vm,
        scratch_shapes=scratch,
        compiler_params=pltpu.CompilerParams(
            collective_id=0, has_side_effects=True, vmem_limit_bytes=60 * 1024 * 1024
        ),
    )(
        lengths, owner.reshape(8, 128), offsets.reshape(8, 128),
        gain_q, gain_kv,
        new_hidden.reshape(32, 896),
        prompt_hidden, w_down.T, w_uq, w_uk, jnp.swapaxes(cache, 1, 2), w_uv, w_out.T,
    )


def solution(mesh):
    in_specs = (
        P("seq", "head"), P("seq", None), P("seq"), P("seq", None, None), P("seq"),
        P(None, "seq", "head"), P("head", None), P(), P(), P(None, "head"),
        P("head", None, None), P("head", None, None), P("head", "seq"),
    )
    return jax.shard_map(
        local, mesh=mesh, in_specs=in_specs, out_specs=P(None, "head", "seq"), check_vma=False
    )
```

time: 102 us -> 79.1 us (0.78)
  Pallas kernels: 89.5 us -> 77.4 us
  other arithmetic: 9.01 us -> 0 us
  local copies, waits for them, and re-layouts: 3.02 us -> 1.47 us
    pallas_call x1, Pallas kernels: 89.5 us -> 77.4 us  [local(): pl.pallas_call(kernel, out_shape=jax.ShapeDtypeStruct((2, 32, 448), BF16)...]
    select_n x5 -> x0, other arithmetic: 2.17 us -> none  [the longest x1 0.75 us: local(): jnp.where(row < 32, jnp.where(lane == 64 + row % 16, 1.0, 0.0) + jnp.wher...]
    cos x2 -> x0, other arithmetic: 2.04 us -> none  [local(): cos, sin = (jnp.cos(angles), jnp.sin(angles))]
    convert_element_type x3 -> x0, other arithmetic: 1.4 us -> none  [the longest x1 1.39 us: local(): ex = (jnp.where(lane == 64 + off // 1024, 1, 0) + jnp.where(lane == 81, p...]
    concatenate x2 -> x0, other arithmetic: 1.34 us -> none  [the longest x1 1.27 us: local(): ctab = jnp.concatenate([cos, cos, -sin, sin], axis=1)]
where the time goes in v2:
time: 79.1 us; the launch traced here: 78.9 us
  Pallas kernels  77.4 us (98%)
  local copies, waits for them, and re-layouts  1.47 us (2%)
    pallas_call x1, Pallas kernels, local(): pl.pallas_call(kernel, out_shape=jax.ShapeDtypeStruct((2, 32, 448), BF16)...  77.4 us

profile of v2, /device:TPU:5, one launch (start us, length us, event | category | flops | bytes accessed | tf_op | source)
XLA Modules:
  0.0 78.9 jit_solution(8172704587790386880)
XLA Ops:
  0.0 77.4 %shard_map.127 = bf16[2,32,448]{2,1,0:T(8,128)(2,1)} custom-call(s32[16]{0:T(128)} %lens.1, s32[8,128]{1,0:T(8,128)} %bitcast.10, s32[8,128]{1,0:T(8,128)} %bitcast.11, bf16[1536]{0:T(1024)(128)(2,1)} %gain_q.1, bf16[512]{0:T(512)(128)(2,1)} %gain_kv.1, bf16[32,896]{1,0:T(8,128)(2,1)} %bitcast.9, bf16[1024,896]{1,0:T(8,128)(2,1)} %hid_h.1, ...), custom_call_target="tpu_custom_call" | custom-call | tf_op jit(solution)/shard_map/pallas_call | solution.py:674
  77.4 1.5 %copy.15 = bf16[2,32,448]{2,1,0:T(8,128)(2,1)} copy(bf16[2,32,448]{2,1,0:T(8,128)(2,1)} %shard_map.127) | data formatting | bytes 114688

commit v3 on v2

--- a/solution.py
+++ b/solution.py
@@ -55,7 +55,7 @@
     npp, npair, npx, npxr, npfin, np_ss, np_rs, ntab,
     part, ps, pr, xs, xr, mine, p_ss, p_rs, x_ss, x_rs,
     disp, slots, d_ss, d_rs, g_ss, g_rs,
-    qls, ql, qs, newk, biasm, acc, m_s, l_s, ob, op,
+    qls, ql, qs, newk, snew, enew, biasm, acc, m_s, l_s, ob, op,
     hog, h_ss, h_rs, ores, opair, opin, op_ss, op_rs, osend, orecv, o_ss, o_rs,
 ):
     i = lax.axis_index("seq")
@@ -162,8 +162,9 @@
 
     c_uv = load(uv_h, uv, lsem.at[4])
     c_wo = load(wo_h, wo, lsem.at[5])
-    def project(t):
-        rows = pl.ds(t * 512, 512)
+    @pl.loop(0, 2)
+    def _(t):
+        rows = pl.ds(pl.multiple_of(t * 512, 512), 512)
         h = hid[rows, :]
         part[rows, 0:512] = nt(h, wd[1536:2048, :]).astype(BF16)
         u = nt(h, wd[2048:2112, :])
@@ -173,9 +174,6 @@
         return remote(
             npx, npxr.at[dx], np_ss.at[dx], np_rs.at[dx], (i, 2 * ((x + dx) % 4) + c)
         )
-
-    project(0)
-    project(1)
 
     def permuted(first, second):
         ids = rs[0:8, :]
@@ -202,7 +200,9 @@
             (i, 2 * ((x + dx) % 4) + c),
         )
 
-    for first, second in ((2, 1), (3, 0)):
+    @pl.loop(0, 2)
+    def _(t):
+        first, second = 2 + t, 1 - t
         both = permuted(2 * ((x + first) % 4) + 1 - c, 2 * ((x + second) % 4) + 1 - c)
         ps[first] = both[0:128].astype(BF16)
         ps[second] = both[128:256].astype(BF16)
@@ -217,8 +217,6 @@
         to = (i + di) % 16
         return remote(tsend.at[to], trecv.at[i], ts_sem.at[di], tr_sem.at[di], (to, j))
 
-    for di in range(1, 16):
-        t_copy(di).start()
     both = permuted(2 * ((x + 2) % 4) + c, 2 * ((x + 1) % 4) + c)
     np_pair.wait_recv()
     npx[...] = (npp[c].astype(F32) + npair[...].astype(F32)).astype(BF16)
@@ -228,6 +226,8 @@
     xs[2] = (both[0:128] + pr[2].astype(F32)).astype(BF16)
     via_copy(0).start()
     via_copy(1).start()
+    for di in range(1, 16):
+        t_copy(di).start()
     p_copy(1).wait_recv()
     up = both[128:256] + pr[1].astype(F32)
     xs[1, 64:128, :] = up[64:128].astype(BF16)
@@ -292,8 +292,8 @@
 
     @pl.loop(0, 4)
     def _(p):
-        two_heads(2 * p)
-        two_heads(2 * p + 1)
+        for q in range(2):
+            two_heads(2 * p + q)
 
     @pl.loop(0, 2)
     def _(t):
@@ -301,6 +301,67 @@
         want = ((n & 31) >> 1) * 32 + (n & 1) * 16 + (n >> 5)
         rows = pl.ds(pl.multiple_of(t * 256, 256), 256)
         qs[rows, :] = nn(one_hot(iota((256, 512), 1) == want), ql[...]).astype(BF16)
+
+    at_src = tsend[i]
+    trecv[i] = at_src
+    for di in range(1, 16):
+        src = (i + 16 - di) % 16
+        remote(tsend.at[src], trecv.at[src], ts_sem.at[di], tr_sem.at[di], (src, j)).wait_recv()
+
+    tall, wide = [], []
+    for s in range(16):
+        cell = trecv[s, 0:1, :].astype(I32)
+        tall.append(one_hot(sub128 == (cell >> 7)))
+        wide.append(one_hot(sub128 == (cell & 127)))
+    taken = nt(jnp.concatenate(tall, axis=1), jnp.concatenate(wide, axis=1))
+    length = jnp.zeros((128, 128), I32)
+    weigh = jnp.where(iota((8, 128), 1) == 81, -128.0, 0.0)
+    weigh = jnp.where(iota((8, 128), 1) == 82, -1.0, weigh)
+    for r in range(16):
+        length = length + jnp.where((sub128 >> 3) == r, lens[r], 0)
+        weigh = weigh + jnp.where(iota((8, 128), 1) == 64 + r, lens[r], 0).astype(F32)
+    seen = (sub128 & 7) * 128 + lane128 < length
+    biasm[...] = jnp.where((taken < 0.5) & seen, 0.0, HIDE)
+
+    snew[...] = nt(qs[...], newk[...])
+    quarter = [one_hot((lane128 >> 5) == r) for r in range(4)]
+
+    def cache_four(t):
+        if True:
+            for r in range(4):
+                k_copy(4 * t + r).wait()
+            rows = pl.ds(pl.multiple_of(t * 128, 128), 128)
+            bias = biasm[pl.ds(pl.multiple_of(t * 32, 32), 32), :]
+            s = [
+                nn(qs[pl.ds(pl.multiple_of(t * 128 + r * 32, 32), 32), 0:576], kc[4 * t + r])
+                for r in range(4)
+            ]
+            s = [
+                jnp.concatenate(
+                    [
+                        s[r][:, g * 128 : (g + 1) * 128] + bias[8 * r + g : 8 * r + g + 1, :]
+                        for r in range(4)
+                    ],
+                    axis=0,
+                )
+                for g in range(8)
+            ]
+            s.append(snew[rows, :])
+            top = jnp.max(functools.reduce(jnp.maximum, s), axis=1, keepdims=True)
+            m = jnp.broadcast_to(top, (128, 128))
+            e = [jnp.exp2(v - m) for v in s]
+            m_s[rows, :] = m
+            l_s[rows, :] = functools.reduce(jnp.add, e)
+            enew[rows, :] = e[8].astype(BF16)
+            e = [v.T.astype(BF16) for v in e[0:8]]
+            val = functools.reduce(
+                jnp.add,
+                [
+                    nn(kc[4 * t + r, 0:512, :], jnp.concatenate([v * quarter[r] for v in e], axis=0))
+                    for r in range(4)
+                ],
+            )
+            acc[rows, :] = val.T
 
     total = mine[...]
     for dx in (1, 3):
@@ -334,66 +395,6 @@
     at_me = pl.ds(pl.multiple_of(i * 16, 16), 16)
     slots[j, at_me, :] = disp[at_me, :]
 
-    at_src = tsend[i]
-    trecv[i] = at_src
-    for di in range(1, 16):
-        src = (i + 16 - di) % 16
-        remote(tsend.at[src], trecv.at[src], ts_sem.at[di], tr_sem.at[di], (src, j)).wait_recv()
-
-    tall, wide = [], []
-    for s in range(16):
-        cell = trecv[s, 0:1, :].astype(I32)
-        tall.append(one_hot(sub128 == (cell >> 7)))
-        wide.append(one_hot(sub128 == (cell & 127)))
-    taken = nt(jnp.concatenate(tall, axis=1), jnp.concatenate(wide, axis=1))
-    length = jnp.zeros((128, 128), I32)
-    weigh = jnp.where(iota((8, 128), 1) == 81, -128.0, 0.0)
-    weigh = jnp.where(iota((8, 128), 1) == 82, -1.0, weigh)
-    for r in range(16):
-        length = length + jnp.where((sub128 >> 3) == r, lens[r], 0)
-        weigh = weigh + jnp.where(iota((8, 128), 1) == 64 + r, lens[r], 0).astype(F32)
-    seen = (sub128 & 7) * 128 + lane128 < length
-    biasm[...] = jnp.where((taken < 0.5) & seen, 0.0, HIDE)
-
-    def cache_part(r):
-        rows = pl.ds(pl.multiple_of(r * 32, 32), 32)
-        s = nn(qs[rows, 0:576], kc[r])
-        b8 = biasm[pl.ds(pl.multiple_of(r * 8, 8), 8), :]
-        s = [s[:, g * 128 : (g + 1) * 128] + b8[g : g + 1, :] for g in range(8)]
-        s.append(nt(qs[rows, :], newk[...]))
-        top = jnp.max(functools.reduce(jnp.maximum, s), axis=1, keepdims=True)
-        m = jnp.broadcast_to(top, (32, 128))
-        e = [jnp.exp2(v - m) for v in s]
-        m_s[rows, :] = m
-        l_s[rows, :] = functools.reduce(jnp.add, e)
-        e = [v.astype(BF16) for v in e]
-        acc[rows, :] = nt(jnp.concatenate(e[0:8], axis=1), kc[r, 0:512, :]) + nn(
-            e[8], newk[:, 0:512]
-        )
-
-    def cache_four(t):
-        for r in range(4):
-            k_copy(4 * t + r).wait()
-        for r in range(4):
-            cache_part(4 * t + r)
-
-    @pl.loop(0, 1)
-    def _(t):
-        cache_four(t)
-
-    for di in range(1, 16):
-        src = (i + 16 - di) % 16
-        remote(
-            disp.at[pl.ds(pl.multiple_of(src * 16, 16), 16), :],
-            slots.at[j, pl.ds(pl.multiple_of(src * 16, 16), 16), :],
-            d_ss.at[di], d_rs.at[di], (src, j),
-        ).wait_recv()
-    marks = slots[j, :, 512:640].astype(F32)
-    left = jnp.sum(marks * weigh[0:1, :], axis=1, keepdims=True)
-    marks = jnp.where(
-        iota((256, 128), 1) == 80, jnp.where(left > 0.5, 0.0, 1.0), marks
-    )
-    slots[j, :, 512:640] = marks.astype(BF16)
 
     def g_half(block, k):
         return slots.at[block, pl.ds(128 * k, 128), :]
@@ -406,20 +407,54 @@
     def g_wait(block, k):
         g_copy(block, k, 0, sib).wait_recv()
 
-    above, below, across = 2 * ((x + 1) % 4), 2 * ((x + 3) % 4), 2 * ((x + 2) % 4)
+    above, below, across = (2 * ((x + d) % 4) + c for d in (1, 3, 2))
     g_sent = []
 
     def g_send(block, k, to):
-        cp = g_copy(block, k, len(g_sent), to)
-        cp.start()
-        g_sent.append(cp)
-
-    g_send(j, 0, above + c)
-    g_send(j, 1, below + c)
-    g_send(j, 1, above + c)
-    g_send(j, 0, below + c)
-    g_send(j, 0, sib)
-    g_send(j, 1, sib)
+        g_sent.append((block, k, len(g_sent), to))
+        g_copy(*g_sent[-1]).start()
+
+    @pl.loop(0, 4)
+    def _(t):
+        cache_four(t)
+
+        @pl.when(t == 0)
+        def _():
+            for di in range(1, 16):
+                src = (i + 16 - di) % 16
+                remote(
+                    disp.at[pl.ds(pl.multiple_of(src * 16, 16), 16), :],
+                    slots.at[j, pl.ds(pl.multiple_of(src * 16, 16), 16), :],
+                    d_ss.at[di], d_rs.at[di], (src, j),
+                ).wait_recv()
+            marks = slots[j, :, 512:640].astype(F32)
+            left = jnp.sum(marks * weigh[0:1, :], axis=1, keepdims=True)
+            marks = jnp.where(
+                iota((256, 128), 1) == 80, jnp.where(left > 0.5, 0.0, 1.0), marks
+            )
+            slots[j, :, 512:640] = marks.astype(BF16)
+            g_send(j, 0, above)
+            g_send(j, 1, below)
+            g_send(j, 0, sib)
+            g_send(j, 1, sib)
+
+        @pl.when(t == 1)
+        def _():
+            g_copy(*g_sent[0]).wait_send()
+            g_copy(*g_sent[1]).wait_send()
+            g_send(j, 1, above)
+            g_send(j, 0, below)
+
+        @pl.when(t == 2)
+        def _():
+            g_wait(below, 0)
+            g_send(below, 0, above)
+            g_wait(above, 1)
+            g_send(above, 1, below)
+            g_send(below, 0, sib)
+            g_send(above, 1, sib)
+
+    acc[...] = acc[...] + nn(enew[...], newk[:, 0:512])
 
     def slot_part(first, second):
         q = qs[...]
@@ -438,45 +473,22 @@
         val = val + nn(jnp.concatenate(e[2:4], axis=1), slots[second, :, 0:512])
         acc[...] = acc[...] * jnp.concatenate([keep] * 4, axis=1) + val
 
-    @pl.loop(1, 2)
+    @pl.loop(0, 4)
     def _(t):
-        cache_four(t)
-
-    g_wait(below + c, 0)
-    g_send(below + c, 0, above + c)
-    g_wait(above + c, 1)
-    g_send(above + c, 1, below + c)
-    g_send(below + c, 0, sib)
-    g_send(above + c, 1, sib)
-
-    @pl.loop(2, 3)
-    def _(t):
-        cache_four(t)
-
-    g_wait(below + c, 1)
-    g_send(below + c, 1, sib)
-    g_wait(above + c, 0)
-    g_send(above + c, 0, sib)
-
-    @pl.loop(3, 4)
-    def _(t):
-        cache_four(t)
-
-    @pl.loop(0, 2)
-    def _(t):
-        chip = 2 * ((x + 3 * t) % 4)
-        for k in range(2):
-            g_wait(chip + 1 - c, k)
-        slot_part(chip + c, chip + 1 - c)
-
-    g_wait(across + c, 0)
-    g_send(across + c, 0, sib)
-    g_wait(across + c, 1)
-    g_send(across + c, 1, sib)
-
-    @pl.loop(0, 2)
-    def _(t):
-        chip = 2 * ((x + 1 + t) % 4)
+        @pl.when(t == 1)
+        def _():
+            g_wait(below, 1)
+            g_send(below, 1, sib)
+            g_wait(above, 0)
+            g_send(above, 0, sib)
+
+        @pl.when(t == 3)
+        def _():
+            for k in range(2):
+                g_wait(across, k)
+                g_send(across, k, sib)
+
+        chip = 2 * ((x + jnp.where(t == 1, 3, jnp.where(t == 2, 1, jnp.where(t == 3, 2, 0)))) % 4)
         for k in range(2):
             g_wait(chip + 1 - c, k)
         slot_part(chip + c, chip + 1 - c)
@@ -512,19 +524,37 @@
 
     h_sent = []
 
-    def h_copy(half, piece, part_at, k, to):
-        ref = hog.at[half, piece]
-        if part_at is not None:
-            ref = hog.at[half, piece, pl.ds(16 * part_at, 16), :]
-        return remote(ref, ref, h_ss.at[k], h_rs.at[half, piece, part_at or 0], (to, j))
-
-    def h_send(half, piece, part_at, to):
-        cp = h_copy(half, piece, part_at, len(h_sent), to)
+    def h_copy(half, piece, k, ss, to):
+        ref = hog.at[half, piece, pl.ds(16 * k, 16), :]
+        return remote(ref, ref, h_ss.at[ss], h_rs.at[half, piece, k], (to, j))
+
+    def h_send(half, piece, k, to):
+        cp = h_copy(half, piece, k, len(h_sent), to)
         cp.start()
         h_sent.append(cp)
 
-    def h_wait(half, piece, part_at=None):
-        h_copy(half, piece, part_at, 0, i).wait_recv()
+    def h_wait(half, piece, k):
+        h_copy(half, piece, k, 0, i).wait_recv()
+
+    def far_first(half, piece):
+        h_send(half, piece, 0, far(half, 1))
+        h_send(half, piece, 1, far(half, 3))
+
+    def far_rest(half, piece):
+        h_send(half, piece, 1, far(half, 1))
+        h_send(half, piece, 0, far(half, 3))
+
+    def far_on(half, n):
+        h_wait(half, cross(half, n, 3), 0)
+        h_send(half, cross(half, n, 3), 0, far(half, 1))
+        h_wait(half, cross(half, n, 1), 1)
+        h_send(half, cross(half, n, 1), 1, far(half, 3))
+
+    def far_end(half, n, f):
+        if f != 1:
+            h_wait(half, cross(half, n, f), 1)
+        if f != 3:
+            h_wait(half, cross(half, n, f), 0)
 
     halves = range(2)
     for half in halves:
@@ -532,33 +562,40 @@
             hog[half, i, :, h * 128 : (h + 1) * 128] = nn(
                 op[(half * 8 + h) * 32 : (half * 8 + h + 1) * 32, :], uv[half * 8 + h]
             ).astype(BF16)
-        for d in (1, 3):
-            h_send(half, i, None, near(half, d))
-        for d in (1, 3):
-            h_send(half, i, None, far(half, d))
-
-    def pass_on(half, n, f, to):
-        piece = cross(half, n, f)
-        h_wait(half, piece)
-        h_send(half, piece, 0 if (f == 3 or (f == 0 and n == 3)) else 1, to)
-
+        h_send(half, i, 0, near(half, 1))
+        h_send(half, i, 1, near(half, 3))
+        h_send(half, i, 1, near(half, 1))
+        h_send(half, i, 0, near(half, 3))
+    for half in halves:
+        far_first(half, i)
+    for half in halves:
+        h_wait(half, near(half, 3), 0)
+        h_send(half, near(half, 3), 0, near(half, 1))
+        h_wait(half, near(half, 1), 1)
+        h_send(half, near(half, 1), 1, near(half, 3))
+    for half in halves:
+        h_wait(half, near(half, 3), 1)
+        far_first(half, near(half, 3))
+        h_wait(half, near(half, 1), 0)
+        far_first(half, near(half, 1))
+    for half in halves:
+        far_on(half, 0)
+    for half in halves:
+        far_rest(half, i)
+    for half in halves:
+        h_wait(half, near(half, 2), 0)
+        h_wait(half, near(half, 2), 1)
+        far_first(half, near(half, 2))
     for n in (3, 1):
         for half in halves:
-            pass_on(half, n, 0, near(half, 4 - n))
-            for d in (1, 3):
-                h_send(half, near(half, n), None, far(half, d))
-    for f in (3, 1):
+            far_on(half, n)
+    for n in (3, 1):
         for half in halves:
-            pass_on(half, 0, f, far(half, 4 - f))
-    for half in halves:
-        h_wait(half, near(half, 2), 0)
-        h_wait(half, near(half, 2), 1)
-        for d in (1, 3):
-            h_send(half, near(half, 2), None, far(half, d))
-    for n in (3, 1):
-        for f in (3, 1):
-            for half in halves:
-                pass_on(half, n, f, far(half, 4 - f))
+            far_rest(half, near(half, n))
+    for half in halves:
+        far_on(half, 2)
+    for half in halves:
+        far_rest(half, near(half, 2))
 
     def o_pair(t):
         return remote(opair.at[t], opin.at[t], op_ss.at[t], op_rs.at[t], (i, sib))
@@ -591,25 +628,26 @@
 
     order = (0, 3, 1, 2)
     rows_at = [(z + dz) % 4 for dz in order]
-    h_wait(1, far(1, 2), 0)
-    h_wait(1, far(1, 2), 1)
-    columns(0, rows_at[0])
-    for t, d in ((1, 3), (2, 1)):
-        h_wait(0, cross(0, 2, d))
-        h_send(0, cross(0, 2, d), 0 if d == 3 else 1, far(0, 4 - d))
-        h_wait(1, cross(1, 2, d))
-        h_send(1, cross(1, 2, d), 0 if d == 3 else 1, far(1, 4 - d))
-        for k in range(2):
-            h_wait(1, cross(1, d, 2), k)
-        columns(t, rows_at[t])
-        onward(t - 1, rows_at[t - 1])
-    for n in range(4):
-        for k in range(2):
-            h_wait(0, cross(0, n, 2), k)
-    for k in range(2):
-        h_wait(1, cross(1, 2, 2), k)
-    columns(3, rows_at[3])
-    onward(2, rows_at[2])
+    @pl.loop(0, 4)
+    def _(t):
+        for at, d in enumerate(order):
+
+            @pl.when(t == at)
+            def _():
+                if d != 0:
+                    for n in range(4):
+                        far_end(0, n, d)
+                for f in (1, 3, 2):
+                    far_end(1, d, f)
+
+        step = jnp.where(t == 1, 3, jnp.where(t == 2, 1, jnp.where(t == 3, 2, 0)))
+        last = jnp.where(t == 2, 3, jnp.where(t == 3, 1, 0))
+        columns(t, (z + step) % 4)
+
+        @pl.when(t > 0)
+        def _():
+            onward(t - 1, (z + last) % 4)
+
     onward(3, rows_at[3])
 
     total = jnp.zeros((64, 448), F32)
@@ -636,7 +674,9 @@
         x_copy(1, k).wait_send()
         x_copy(3, k).wait_send()
         via_copy(k).wait_send()
-    for cp in g_sent + h_sent:
+    for one in g_sent[2:]:
+        g_copy(*one).wait_send()
+    for cp in h_sent:
         cp.wait_send()
     for t in range(4):
         o_pair(t).wait_send()
@@ -665,9 +705,9 @@
         S((4,)), S((4,)), S((8,)), S((8,)),
         V((256, 640), BF16), V((8, 256, 640), BF16), S((16,)), S((16,)), S((14,)), S((8, 2)),
         V((32, 1536), BF16), V((512, 640), BF16), V((512, 640), BF16), V((128, 640), BF16),
-        V((128, 128), F32), V((512, 512), F32), V((512, 128), F32), V((512, 128), F32),
+        V((512, 128), F32), V((512, 128), BF16), V((128, 128), F32), V((512, 512), F32), V((512, 128), F32), V((512, 128), F32),
         V((512, 512), BF16), V((512, 512), BF16),
-        V((2, 16, 32, 1024), BF16), S((40,)), S((2, 16, 2)),
+        V((2, 16, 32, 1024), BF16), S((60,)), S((2, 16, 2)),
         V((4, 128, 512), F32), V((4, 64, 512), BF16), V((4, 64, 512), BF16), S((4,)), S((4,)),
         V((4, 64, 512), BF16), V((4, 64, 512), BF16), S((4,)), S((4,)),
     ]

time: 79.1 us -> 77.3 us (0.977)
  Pallas kernels: 77.4 us -> 75.4 us
    pallas_call x1, Pallas kernels: 77.4 us -> 75.4 us  [local(): pl.pallas_call(kernel, out_shape=jax.ShapeDtypeStruct((2, 32, 448), BF16)...]
where the time goes in v3:
time: 77.3 us; the launch traced here: 76.8 us
  Pallas kernels  75.4 us (98%)
  local copies, waits for them, and re-layouts  1.47 us (2%)
    pallas_call x1, Pallas kernels, local(): pl.pallas_call(kernel, out_shape=jax.ShapeDtypeStruct((2, 32, 448), BF16)...  75.4 us

profile of v3, /device:TPU:5, one launch (start us, length us, event | category | flops | bytes accessed | tf_op | source)
XLA Modules:
  0.0 76.8 jit_solution(2294414697581485585)
XLA Ops:
  0.0 75.4 %shard_map.127 = bf16[2,32,448]{2,1,0:T(8,128)(2,1)} custom-call(s32[16]{0:T(128)} %lens.1, s32[8,128]{1,0:T(8,128)} %bitcast.10, s32[8,128]{1,0:T(8,128)} %bitcast.11, bf16[1536]{0:T(1024)(128)(2,1)} %gain_q.1, bf16[512]{0:T(512)(128)(2,1)} %gain_kv.1, bf16[32,896]{1,0:T(8,128)(2,1)} %bitcast.9, bf16[1024,896]{1,0:T(8,128)(2,1)} %hid_h.1, ...), custom_call_target="tpu_custom_call" | custom-call | tf_op jit(solution)/shard_map/pallas_call | solution.py:714
  75.4 1.5 %copy.15 = bf16[2,32,448]{2,1,0:T(8,128)(2,1)} copy(bf16[2,32,448]{2,1,0:T(8,128)(2,1)} %shard_map.127) | data formatting | bytes 114688

commit v4 on v3

--- a/solution.py
+++ b/solution.py
@@ -47,13 +47,13 @@
 
 
 def kernel(
-    lens, own_r, off_r, gain_q, gain_kv, newh,
+    lens, own_h, off_h, gain_q_h, gain_kv_h, newh_h,
     hid_h, wd_h, uq_h, uk_h, cache_h, uv_h, wo_h,
     out,
-    hid, wd, uq, uk, kc, uv, wo, lsem, ksem,
+    own_r, off_r, gain_q, gain_kv, newh, hid, wd, uq, uk, kc, uv, wo, lsem, ksem,
     rs, feat, tsend, trecv, ts_sem, tr_sem,
     npp, npair, npx, npxr, npfin, np_ss, np_rs, ntab,
-    part, ps, pr, xs, xr, mine, p_ss, p_rs, x_ss, x_rs,
+    part, ps, pr, xs, xr, own, p_ss, p_rs, x_ss, x_rs,
     disp, slots, d_ss, d_rs, g_ss, g_rs,
     qls, ql, qs, newk, snew, enew, biasm, acc, m_s, l_s, ob, op,
     hog, h_ss, h_rs, ores, opair, opin, op_ss, op_rs, osend, orecv, o_ss, o_rs,
@@ -77,15 +77,22 @@
             device_id=dev, device_id_type=MESH,
         )
 
+    c_own = load(own_h, own_r, lsem.at[6])
+    c_off = load(off_h, off_r, lsem.at[7])
+    c_wd = load(wd_h, wd, lsem.at[0])
+    c_new = load(newh_h, newh, lsem.at[8])
+    c_hid = load(hid_h, hid, lsem.at[1])
+    c_gq = load(gain_q_h, gain_q, lsem.at[9])
+    c_gkv = load(gain_kv_h, gain_kv, lsem.at[10])
+
     barrier = pltpu.get_barrier_semaphore()
     for dj in range(1, 8):
         pl.semaphore_signal(barrier, inc=1, device_id=(i, (j + dj) % 8), device_id_type=MESH)
     for di in range(1, 16):
         pl.semaphore_signal(barrier, inc=1, device_id=((i + di) % 16, j), device_id_type=MESH)
 
-    c_wd = load(wd_h, wd, lsem.at[0])
-    c_hid = load(hid_h, hid, lsem.at[1])
-
+    c_own.wait()
+    c_off.wait()
     sub128 = iota((128, 128), 0)
     lane128 = iota((128, 128), 1)
     sub16 = iota((16, 128), 0)
@@ -144,6 +151,7 @@
     ntab[1] = jnp.where((lane32 & 63) < 32, -1.0, 1.0) * jnp.sin(angle)
 
     c_wd.wait()
+    c_new.wait()
     c_uq = load(uq_h, uq, lsem.at[2])
     c_uk = load(uk_h, uk, lsem.at[3])
     npp[0] = nt(newh[...], wd[0:1152, :]).astype(BF16)
@@ -217,28 +225,36 @@
         to = (i + di) % 16
         return remote(tsend.at[to], trecv.at[i], ts_sem.at[di], tr_sem.at[di], (to, j))
 
-    both = permuted(2 * ((x + 2) % 4) + c, 2 * ((x + 1) % 4) + c)
-    np_pair.wait_recv()
-    npx[...] = (npp[c].astype(F32) + npair[...].astype(F32)).astype(BF16)
-    for dx in (2, 1, 3):
-        npx_copy(dx).start()
-    p_copy(2).wait_recv()
-    xs[2] = (both[0:128] + pr[2].astype(F32)).astype(BF16)
-    via_copy(0).start()
-    via_copy(1).start()
-    for di in range(1, 16):
-        t_copy(di).start()
-    p_copy(1).wait_recv()
-    up = both[128:256] + pr[1].astype(F32)
-    xs[1, 64:128, :] = up[64:128].astype(BF16)
-    x_copy(1, 1).start()
-    both = permuted(2 * ((x + 3) % 4) + c, 2 * x + c)
+    @pl.loop(0, 2)
+    def _(t):
+        first, second = 2 + t, (1 - t) % 4
+        both = permuted(2 * ((x + first) % 4) + c, 2 * ((x + second) % 4) + c)
+        own[first] = both[0:128]
+        own[second] = both[128:256]
+
+        @pl.when(t == 0)
+        def _():
+            np_pair.wait_recv()
+            npx[...] = (npp[c].astype(F32) + npair[...].astype(F32)).astype(BF16)
+            for dx in (2, 1, 3):
+                npx_copy(dx).start()
+            p_copy(2).wait_recv()
+            xs[2] = (own[2] + pr[2].astype(F32)).astype(BF16)
+            via_copy(0).start()
+            via_copy(1).start()
+            for di in range(1, 16):
+                t_copy(di).start()
+            p_copy(1).wait_recv()
+            own[1] = own[1] + pr[1].astype(F32)
+            xs[1, 64:128, :] = own[1, 64:128, :].astype(BF16)
+            x_copy(1, 1).start()
+
     p_copy(3).wait_recv()
-    down = both[0:128] + pr[3].astype(F32)
-    xs[3, 0:64, :] = down[0:64].astype(BF16)
+    own[3] = own[3] + pr[3].astype(F32)
+    xs[3, 0:64, :] = own[3, 0:64, :].astype(BF16)
     x_copy(3, 0).start()
     p_copy(0).wait_recv()
-    mine[...] = both[128:256] + pr[0].astype(F32)
+    own[0] = own[0] + pr[0].astype(F32)
 
     total = npx[...].astype(F32)
     for dx in (1, 3, 2):
@@ -248,15 +264,17 @@
     np_swap = remote(npfin.at[c], npfin.at[c], np_ss.at[4], np_rs.at[4], (i, sib))
     np_swap.start()
     via_copy(0).wait_recv()
-    xs[1, 0:64, :] = (up[0:64] + xr[2, 0:64, :].astype(F32)).astype(BF16)
+    xs[1, 0:64, :] = (own[1, 0:64, :] + xr[2, 0:64, :].astype(F32)).astype(BF16)
     x_copy(1, 0).start()
     via_copy(1).wait_recv()
-    xs[3, 64:128, :] = (down[64:128] + xr[2, 64:128, :].astype(F32)).astype(BF16)
+    xs[3, 64:128, :] = (own[3, 64:128, :] + xr[2, 64:128, :].astype(F32)).astype(BF16)
     x_copy(3, 1).start()
     np_swap_in = remote(npfin.at[1 - c], npfin.at[1 - c], np_ss.at[4], np_rs.at[4], (i, sib))
     np_swap_in.wait_recv()
 
     unit = LOG2E / (NOPE + ROPE) ** 0.5
+    c_gq.wait()
+    c_gkv.wait()
     low32 = iota((32, 128), 1) < 64
     q_in = jnp.concatenate([npfin[0], npfin[1, :, 0:384]], axis=1).astype(F32)
     q_in = q_in * lax.rsqrt(jnp.mean(q_in * q_in, axis=1, keepdims=True) + 1e-6) * gain_q[...].astype(F32).reshape(1, QRANK)
@@ -363,7 +381,7 @@
             )
             acc[rows, :] = val.T
 
-    total = mine[...]
+    total = own[0]
     for dx in (1, 3):
         x_copy(dx, 0).wait_recv()
         x_copy(dx, 1).wait_recv()
@@ -558,10 +576,16 @@
 
     halves = range(2)
     for half in halves:
-        for h in range(8):
-            hog[half, i, :, h * 128 : (h + 1) * 128] = nn(
-                op[(half * 8 + h) * 32 : (half * 8 + h + 1) * 32, :], uv[half * 8 + h]
-            ).astype(BF16)
+
+        @pl.loop(0, 2)
+        def _(t):
+            for h in range(4):
+                at = t * 4 + h
+                rows = pl.ds(pl.multiple_of((half * 8 + at) * 32, 32), 32)
+                hog[half, i, :, pl.ds(pl.multiple_of(at * 128, 128), 128)] = nn(
+                    op[rows, :], uv[half * 8 + at]
+                ).astype(BF16)
+
         h_send(half, i, 0, near(half, 1))
         h_send(half, i, 1, near(half, 3))
         h_send(half, i, 1, near(half, 1))
@@ -695,13 +719,14 @@
     V = pltpu.VMEM
     S = pltpu.SemaphoreType.DMA
     scratch = [
+        V((8, 128), I32), V((8, 128), I32), V((QRANK,), BF16), V((LATENT,), BF16), V((32, 896), BF16),
         V((1024, 896), BF16), V((2112, 896), BF16), V((1536, 3072), BF16), V((16, 128, 512), BF16),
-        V((16, 576, 1024), BF16), V((16, 512, 128), BF16), V((448, 2048), BF16), S((6,)), S((16,)),
+        V((16, 576, 1024), BF16), V((16, 512, 128), BF16), V((448, 2048), BF16), S((11,)), S((16,)),
         V((16, 128), I32), V((128, 128), F32), V((16, 8, 128), F32), V((16, 8, 128), F32), S((16,)), S((16,)),
         V((2, 32, 1152), BF16), V((32, 1152), BF16), V((32, 1152), BF16), V((4, 32, 1152), BF16),
         V((2, 32, 1152), BF16), S((5,)), S((5,)), V((2, 32, 128), F32),
         V((1024, 640), BF16), V((4, 128, 640), BF16), V((4, 128, 640), BF16),
-        V((4, 128, 640), BF16), V((4, 128, 640), BF16), V((128, 640), F32),
+        V((4, 128, 640), BF16), V((4, 128, 640), BF16), V((4, 128, 640), F32),
         S((4,)), S((4,)), S((8,)), S((8,)),
         V((256, 640), BF16), V((8, 256, 640), BF16), S((16,)), S((16,)), S((14,)), S((8, 2)),
         V((32, 1536), BF16), V((512, 640), BF16), V((512, 640), BF16), V((128, 640), BF16),
@@ -714,7 +739,7 @@
     return pl.pallas_call(
         kernel,
         out_shape=jax.ShapeDtypeStruct((2, 32, 448), BF16),
-        in_specs=[pl.BlockSpec(memory_space=pltpu.SMEM)] + [vm] * 5 + [hb] * 7,
+        in_specs=[pl.BlockSpec(memory_space=pltpu.SMEM)] + [hb] * 12,
         out_specs=vm,
         scratch_shapes=scratch,
         compiler_params=pltpu.CompilerParams(

time: 77.3 us -> 76.8 us (level)
  no operation moved by 1% of the time
where the time goes in v4:
time: 76.8 us; the launch traced here: 76.6 us
  Pallas kernels  75.1 us (98%)
  local copies, waits for them, and re-layouts  1.47 us (2%)
    pallas_call x1, Pallas kernels, local(): pl.pallas_call(kernel, out_shape=jax.ShapeDtypeStruct((2, 32, 448), BF16)...  75.1 us

profile of v4, /device:TPU:5, one launch (start us, length us, event | category | flops | bytes accessed | tf_op | source)
XLA Modules:
  0.0 76.6 jit_solution(13021833778741127212)
XLA Ops:
  0.0 75.1 %shard_map.127 = bf16[2,32,448]{2,1,0:T(8,128)(2,1)} custom-call(s32[16]{0:T(128)} %lens.1, s32[8,128]{1,0:T(8,128)} %bitcast.10, s32[8,128]{1,0:T(8,128)} %bitcast.11, bf16[1536]{0:T(1024)(128)(2,1)} %gain_q_h.1, bf16[512]{0:T(512)(128)(2,1)} %gain_kv_h.1, bf16[32,896]{1,0:T(8,128)(2,1)} %bitcast.9, bf16[1024,896]{1,0:T(8,128)(2,1)} %hid_h.1, ...), custom_call_target="tpu_custom_call" | custom-call | tf_op jit(solution)/shard_map/pallas_call | solution.py:739
  75.1 1.5 %copy.15 = bf16[2,32,448]{2,1,0:T(8,128)(2,1)} copy(bf16[2,32,448]{2,1,0:T(8,128)(2,1)} %shard_map.127) | data formatting | bytes 114688

commit v5 on v4

--- a/solution.py
+++ b/solution.py
@@ -665,14 +665,9 @@
                     far_end(1, d, f)
 
         step = jnp.where(t == 1, 3, jnp.where(t == 2, 1, jnp.where(t == 3, 2, 0)))
-        last = jnp.where(t == 2, 3, jnp.where(t == 3, 1, 0))
-        columns(t, (z + step) % 4)
-
-        @pl.when(t > 0)
-        def _():
-            onward(t - 1, (z + last) % 4)
-
-    onward(3, rows_at[3])
+        row = (z + step) % 4
+        columns(t, row)
+        onward(t, row)
 
     total = jnp.zeros((64, 448), F32)
     for dx in range(1, 4):

time: 76.8 us -> 77.9 us (1.014)
  Pallas kernels: 75.1 us -> 76.2 us
    pallas_call x1, Pallas kernels: 75.1 us -> 76.2 us  [local(): pl.pallas_call(kernel, out_shape=jax.ShapeDtypeStruct((2, 32, 448), BF16)...]
where the time goes in v5:
time: 77.9 us; the launch traced here: 77.7 us
  Pallas kernels  76.2 us (98%)
  local copies, waits for them, and re-layouts  1.47 us (2%)
    pallas_call x1, Pallas kernels, local(): pl.pallas_call(kernel, out_shape=jax.ShapeDtypeStruct((2, 32, 448), BF16)...  76.2 us

profile of v5, /device:TPU:5, one launch (start us, length us, event | category | flops | bytes accessed | tf_op | source)
XLA Modules:
  0.0 77.7 jit_solution(14952589091105590142)
XLA Ops:
  0.0 76.2 %shard_map.127 = bf16[2,32,448]{2,1,0:T(8,128)(2,1)} custom-call(s32[16]{0:T(128)} %lens.1, s32[8,128]{1,0:T(8,128)} %bitcast.10, s32[8,128]{1,0:T(8,128)} %bitcast.11, bf16[1536]{0:T(1024)(128)(2,1)} %gain_q_h.1, bf16[512]{0:T(512)(128)(2,1)} %gain_kv_h.1, bf16[32,896]{1,0:T(8,128)(2,1)} %bitcast.9, bf16[1024,896]{1,0:T(8,128)(2,1)} %hid_h.1, ...), custom_call_target="tpu_custom_call" | custom-call | tf_op jit(solution)/shard_map/pallas_call | solution.py:734
  76.3 1.5 %copy.15 = bf16[2,32,448]{2,1,0:T(8,128)(2,1)} copy(bf16[2,32,448]{2,1,0:T(8,128)(2,1)} %shard_map.127) | data formatting | bytes 114688
